TPU v7x, 256 devices: a whole 4x4x8 slice. The times are simulated.
256 devices in a mesh: leaf: 64 (over x, z, core), cpl: 4 (over y).
Axes of the slice: x: 4, y: 4, z: 8, core: 2. Of those that a mesh axis runs over, the one named last changes fastest.
Arguments:
- vectors: bfloat16 [65536, 64], P('leaf'), may hold values from -6 to 6
- embeddings: bfloat16 [65536, 64], P('leaf'), may hold values from -2 to 2
- basis: bfloat16 [65536, 64], P('leaf'), may hold values from -0.75 to 0.75
- transfer: bfloat16 [1984, 64, 64], P('leaf'), may hold values from -0.5 to 0.5
- coupling: bfloat16 [65536, 64, 64], P(('leaf', 'cpl')), may hold values from -0.125 to 0.125
- top_transfer: bfloat16 [62, 64, 64], replicated, may hold values from -0.5 to 0.5
- top_coupling: bfloat16 [62, 64, 64], replicated, may hold values from -3 to 3
- send_boxes: int32 [64, 4, 128], P('leaf', 'cpl'), may hold values from 0 to 30
- block_slot: int32 [65536], P(('leaf', 'cpl')), may hold values from 0 to 127, as said below
- block_target: int32 [65536], P(('leaf', 'cpl')), may hold values from 0 to 31, as said below
Outputs:
- potentials: float32 [65536, 64], P(('leaf', 'cpl'))
Inputs may be any that keep to these rules, and one draw needn't show every extreme that they name: block_slot of a block is a slot p * 2 + k received from leaf device p. Of the 2 slots from one device to another, the ones that live blocks read come first; one device reads all 128 slots. `block_target`: A live block adds to a box at the same level of its subtree as the box that its slot carries; 31 marks an empty block. On every leaf device, one cpl index holds no empty block.
All inputs are finite; a program needn't handle non-finite values.
Results may differ from a plain program's by a relative error of at most 0.0029.
Values may be sent and summed in bfloat16 or wider, within the bound.
A program may use at most 128 MiB of HBM per device.

v0:
```python
import jax
import jax.numpy as jnp
from jax import lax
from jax.sharding import PartitionSpec as P

RANK = 64
NRHS = 64
EMB = 64
LEAF = 64
B_DEV = 16


full_precision = lax.Precision.HIGHEST
sqrt_three = 1.7320508075688772
block_rows = 128


def with_halo(x, sides, width):
    for axis, dim in sides:
        size, length = (lax.axis_size(axis), x.shape[dim])
        up = [(i, (i + 1) % size) for i in range(size - 1)]
        down = [(j, i) for i, j in up]
        last = lax.slice_in_dim(x, length - width, length, axis=dim)
        initial = lax.slice_in_dim(x, 0, width, axis=dim)
        before = lax.ppermute(last, axis, up)
        after = lax.ppermute(initial, axis, down)
        x = jnp.concatenate([before, x, after], axis=dim)
    return x


def matern_block(own_rows, other_rows):
    inner_products = jnp.einsum(
        "bie,bje->bij", own_rows, other_rows, preferred_element_type=jnp.float32
    )
    own_wide = own_rows.astype(jnp.float32)
    other_wide = other_rows.astype(jnp.float32)
    own_norms = jnp.sum(own_wide * own_wide, axis=-1)
    other_norms = jnp.sum(other_wide * other_wide, axis=-1)
    distance = jnp.sqrt(
        jnp.maximum(own_norms[:, :, None] + other_norms[:, None, :] - 2.0 * inner_products, 0.0)
    )
    return ((1.0 + sqrt_three * distance) * jnp.exp(-sqrt_three * distance)).astype(jnp.bfloat16)


def lift_up(matrices, coefficients):
    return jnp.einsum(
        "brs,brn->bsn", matrices.astype(jnp.float32), coefficients, precision=full_precision
    )


def push_down(matrices, fields):
    return jnp.einsum(
        "brs,bsn->brn", matrices.astype(jnp.float32), fields, precision=full_precision
    )


def pick_row(matrix_table, row_index):
    return lax.dynamic_index_in_dim(matrix_table, row_index, 0, keepdims=False)


def body(
    vectors,
    embeddings,
    basis,
    transfer,
    coupling,
    top_transfer,
    top_coupling,
    send_boxes,
    block_slot,
    block_target,
):
    leaf_count = lax.axis_size("leaf")
    height = leaf_count.bit_length() - 1
    local_depth = B_DEV.bit_length() - 1
    box_count = 2 * B_DEV - 1
    position = lax.axis_index("leaf")
    column = lax.axis_index("cpl")
    cpl_count = lax.axis_size("cpl")
    share_leaves = B_DEV // cpl_count
    leaf_vectors = vectors.reshape(B_DEV, LEAF, NRHS)
    leaf_basis = basis.reshape(B_DEV, LEAF, RANK)
    coef_levels = [
        jnp.einsum("bir,bin->brn", leaf_basis, leaf_vectors, preferred_element_type=jnp.float32)
    ]
    for stratum in range(local_depth - 1, -1, -1):
        first_row = (1 << stratum + 1) - 1
        raised = lift_up(transfer[first_row : first_row + (2 << stratum)], coef_levels[0])
        coef_levels.insert(0, raised[0::2] + raised[1::2])
    box_coef = jnp.concatenate(coef_levels, axis=0)
    root_up = lift_up(transfer[0:1], box_coef[0:1])[0]
    fields = {}
    raised = lax.all_gather(root_up[None], "leaf", axis=0, tiled=True)
    top_coefs = {}
    for stratum in range(height - 1, 0, -1):
        parents = raised[0::2] + raised[1::2]
        top_coefs[stratum] = parents
        if stratum > 1:
            first_row = (1 << stratum) - 2
            raised = lift_up(top_transfer[first_row : first_row + (1 << stratum)], parents)
    for stratum in range(1, height):
        within = position >> height - stratum
        sibling = pick_row(top_coefs[stratum], within ^ 1)
        fields[stratum] = push_down(
            pick_row(top_coupling, (1 << stratum) - 2 + within)[None], sibling[None]
        )[0]
    top_down = fields[1]
    for stratum in range(2, height):
        node_index = (1 << stratum) - 2 + (position >> height - stratum)
        top_down = (
            fields[stratum] + push_down(pick_row(top_transfer, node_index)[None], top_down[None])[0]
        )
    rounded = box_coef.reshape(box_count, RANK * NRHS).astype(jnp.bfloat16)
    outgoing_rows = jnp.take(rounded, send_boxes.reshape(-1), axis=0)
    received = lax.all_to_all(outgoing_rows, "leaf", split_axis=0, concat_axis=0, tiled=True)
    partial_value = jnp.zeros((box_count, RANK * NRHS), jnp.float32)
    target_rows = jnp.arange(box_count, dtype=jnp.int32)[:, None]
    for offset in range(0, coupling.shape[0], block_rows):
        matrices = coupling[offset : offset + block_rows]
        sources = jnp.take(received, block_slot[offset : offset + block_rows], axis=0).reshape(
            -1, RANK, NRHS
        )
        products = jnp.einsum(
            "brs,bsn->brn", matrices, sources, preferred_element_type=jnp.float32
        ).reshape(-1, RANK * NRHS)
        selector = (block_target[offset : offset + block_rows][None, :] == target_rows).astype(
            jnp.bfloat16
        )
        upper = lax.optimization_barrier(products.astype(jnp.bfloat16))
        lower = (products - upper.astype(jnp.float32)).astype(jnp.bfloat16)
        partial_value = (
            partial_value
            + jnp.dot(selector, upper, preferred_element_type=jnp.float32)
            + jnp.dot(selector, lower, preferred_element_type=jnp.float32)
        )
    summed = lax.psum(partial_value, "cpl").reshape(box_count, RANK, NRHS)
    current = summed[0:1] + push_down(transfer[0:1], top_down[None])
    for stratum in range(1, local_depth + 1):
        first_row = (1 << stratum) - 1
        current = summed[first_row : first_row + (1 << stratum)] + push_down(
            transfer[first_row : first_row + (1 << stratum)], jnp.repeat(current, 2, axis=0)
        )
    leaf_down = lax.dynamic_slice_in_dim(current, column * share_leaves, share_leaves, 0)
    mine_basis = lax.dynamic_slice_in_dim(leaf_basis, column * share_leaves, share_leaves, 0)
    far_part = jnp.einsum(
        "bir,brn->bin",
        mine_basis,
        leaf_down.astype(jnp.bfloat16),
        preferred_element_type=jnp.float32,
    )
    stacked = jnp.concatenate([vectors, embeddings], axis=1)
    padded = with_halo(stacked, (("leaf", 0),), LEAF)
    window = lax.dynamic_slice_in_dim(
        padded, column * share_leaves * LEAF, (share_leaves + 2) * LEAF, 0
    ).reshape(share_leaves + 2, LEAF, NRHS + EMB)
    near_vectors = window[:, :, :NRHS]
    near_embed = window[:, :, NRHS:]
    own_embed = near_embed[1 : share_leaves + 1]
    near_part = jnp.zeros((share_leaves, LEAF, NRHS), jnp.float32)
    for offset in range(3):
        kernel = matern_block(own_embed, near_embed[offset : offset + share_leaves])
        near_part = near_part + jnp.einsum(
            "bij,bjn->bin",
            kernel,
            near_vectors[offset : offset + share_leaves],
            preferred_element_type=jnp.float32,
        )
    return (far_part + near_part).reshape(share_leaves * LEAF, NRHS)


def solution(mesh):
    placed = (
        P("leaf", None),
        P("leaf", None),
        P("leaf", None),
        P("leaf", None, None),
        P(("leaf", "cpl"), None, None),
        P(),
        P(),
        P("leaf", "cpl", None),
        P(("leaf", "cpl")),
        P(("leaf", "cpl")),
    )
    return jax.shard_map(
        body, mesh=mesh, in_specs=placed, out_specs=P(("leaf", "cpl"), None), check_vma=False
    )
```

profile of v0, /device:TPU:1, one launch (start us, length us, event | category | flops | bytes accessed | tf_op | source)
XLA Modules:
  0.0 215.2 jit_solution(14483411201479575541)
XLA Ops:
  7.4 1.2 copy.63
  8.5 1.2 copy.103
  10.0 1.4 convolution_bitcast_fusion.5
  11.4 1.2 convolution_bitcast_fusion.8
  12.6 1.1 convolution_bitcast_fusion.11
  13.7 1.0 convolution_bitcast_fusion.13
  14.7 0.9 convolution_bitcast_fusion.15
  17.0 1.2 gather_fusion
  20.2 2.1 broadcast_select_fusion
  22.3 13.2 %all-to-all-start = ((bf16[64,2,4096]{2,1,0:T(2,128)(2,1)}), bf16[64,2,4096]{2,1,0:T(2,128)(2,1)}, u32[]{:S(2)}, u32[]{:S(2)}) async-start(bf16[64,2,4096]{2,1,0:T(2,128)(2,1)} %broadcast_select_fusion), calls=%async_computation | async-start | bytes 2097152 | tf_op jit(solution)/shard_map/all_to_all | solution.py:115
  35.7 3.5 %collective-permute-start = (bf16[64,128]{0,1:T(8,128)(2,1)S(1)}, bf16[64,128]{0,1:T(8,128)(2,1)S(1)}, u32[]{:S(2)}, u32[]{:S(2)}) collective-permute-start(bf16[64,128]{0,1:T(8,128)(2,1)S(1)} %get-tuple-element.18), channel_id=1, source_target_pairs={{0,4},{4,8},{8,12},{12,16},{16,20},{20,24},{24,28},{28,32},{32,36}... | collective-permute-start | bytes 49160 | tf_op jit(solution)/shard_map/ppermute | solution.py:25
  39.3 2.1 collective-permute-start.1
  41.4 1.7 fusion.140
  43.2 3.8 %copy.104 = bf16[128,64,64]{2,1,0:T(8,128)(2,1)} copy(bf16[128,64,64]{0,2,1:T(8,128)(2,1)S(1)} %get-tuple-element.16) | data formatting | bytes 2097152
  47.0 3.7 %copy.105 = bf16[128,64,64]{2,1,0:T(8,128)(2,1)} copy(bf16[128,64,64]{0,2,1:T(8,128)(2,1)S(1)} %get-tuple-element.15) | data formatting | bytes 2097152
  50.7 6.6 %collective-permute-done = bf16[64,128]{0,1:T(8,128)(2,1)S(1)} collective-permute-done((bf16[64,128]{0,1:T(8,128)(2,1)S(1)}, bf16[64,128]{0,1:T(8,128)(2,1)S(1)}, u32[]{:S(2)}, u32[]{:S(2)}) %collective-permute-start) | collective-permute-done | bytes 16416 | tf_op jit(solution)/shard_map/ppermute | solution.py:25
  57.3 4.4 %collective-permute-done.1 = bf16[64,128]{0,1:T(8,128)(2,1)S(1)} collective-permute-done((bf16[64,128]{0,1:T(8,128)(2,1)S(1)}, bf16[64,128]{0,1:T(8,128)(2,1)S(1)}, u32[]{:S(2)}, u32[]{:S(2)}) %collective-permute-start.1) | collective-permute-done | bytes 16416 | tf_op jit(solution)/shard_map/ppermute | solution.py:26
  63.3 1.0 convolution_add_fusion.3
  64.3 36.4 %all-gather.3.cloned.1.call-done = f32[4096,64]{1,0:T(8,128)} async-done(((f32[64,64]{1,0:T(8,128)}), f32[4096,64]{1,0:T(8,128)}) %all-gather.3.cloned.1.call-update) | async-done | bytes 1048592 | tf_op jit(solution)/shard_map/all_gather | solution.py:93
  100.7 2.7 %fusion.139 = (f32[32,64,64]{2,1,0:T(8,128)}, f32[32,64,64]{2,1,0:T(8,128)S(1)}) fusion(f32[64,64,64]{2,1,0:T(8,128)} %bitcast.139), kind=kLoop, calls=%fused_computation.208 | loop fusion | bytes 2097152 | tf_op jit(solution)/shard_map/slice | solution.py:96
  103.8 1.6 copy.107
  105.6 1.0 copy-done.9
  109.5 1.5 all_to_all.7
  111.0 1.2 gather_fusion.1
  112.2 1.2 broadcast_select_fusion.2
  113.4 1.6 copy.74
  115.0 4.4 %copy.76 = bf16[128,64,64]{1,2,0:T(8,128)(2,1)} copy(bf16[128,64,64]{0,2,1:T(8,128)(2,1)S(1)} %bitcast.137) | data formatting | bytes 2097152 | tf_op jit(solution)/shard_map/reshape | solution.py:120
  119.4 5.5 %convolution_bitcast_fusion.1 = f32[128,64,64]{1,2,0:T(8,128)} fusion(bf16[128,64,64]{1,2,0:T(8,128)(2,1)} %copy.76, bf16[128,64,64]{2,1,0:T(8,128)(2,1)} %copy.104), kind=kOutput, calls=%fused_computation.7 | convolution fusion | flops 67108864 | bytes 4194304 | tf_op jit(solution)/shard_map/brs,bsn->brn/dot_general | solution.py:123
  124.9 5.3 %copy.77 = f32[128,64,64]{0,2,1:T(8,128)} copy(f32[128,64,64]{1,2,0:T(8,128)} %convolution_bitcast_fusion.1) | data formatting | bytes 4194304 | tf_op jit(solution)/shard_map/brs,bsn->brn/dot_general | solution.py:123
  130.2 1.8 bitcast_convert_fusion.1
  132.4 1.2 fusion.1
  133.6 1.3 fusion.106
  134.8 1.2 gather_fusion.2
  136.2 1.4 copy.78
  137.6 5.6 %copy.80 = bf16[128,64,64]{1,2,0:T(8,128)(2,1)} copy(bf16[128,64,64]{0,2,1:T(8,128)(2,1)} %bitcast.138) | data formatting | bytes 2097152 | tf_op jit(solution)/shard_map/reshape | solution.py:120
  143.1 4.8 %convolution_bitcast_fusion = f32[128,64,64]{1,2,0:T(8,128)} fusion(bf16[128,64,64]{1,2,0:T(8,128)(2,1)} %copy.80, bf16[128,64,64]{2,1,0:T(8,128)(2,1)S(1)} %copy-done.2), kind=kOutput, calls=%fused_computation.6 | convolution fusion | flops 67108864 | bytes 4194304 | tf_op jit(solution)/shard_map/brs,bsn->brn/dot_general | solution.py:123
  147.9 4.5 %copy.81 = f32[128,64,64]{0,2,1:T(8,128)S(1)} copy(f32[128,64,64]{1,2,0:T(8,128)} %convolution_bitcast_fusion) | data formatting | bytes 4194304 | tf_op jit(solution)/shard_map/brs,bsn->brn/dot_general | solution.py:123
  152.8 1.0 copy-done.4
  154.8 1.3 convolution_add_fusion
  157.6 0.9 convolution_add_fusion.8
  158.5 0.9 fusion.74
  159.4 0.9 fusion.76
  162.1 37.3 %all-reduce.2.cloned.1.call-done = f32[31,4096]{1,0:T(8,128)} async-done(((f32[31,4096]{1,0:T(8,128)}), f32[31,4096]{1,0:T(8,128)}) %all-reduce.2.cloned.1.call-update) | async-done | bytes 507920 | tf_op jit(solution)/shard_map/psum | solution.py:136
  199.4 0.9 slice_reduce_fusion
  200.5 0.9 slice.231
  201.6 0.9 slice.230
  202.8 1.0 slice.229
  206.1 1.0 convolution_add_fusion.5
  (110 shorter events, 17.1 us)
Async XLA Ops:
  7.4 148.8 %copy-start = (bf16[62,64,64]{2,1,0:T(8,128)(2,1)S(1)}, bf16[62,64,64]{2,1,0:T(8,128)(2,1)}, u32[]{:S(2)}) copy-start(bf16[62,64,64]{2,1,0:T(8,128)(2,1)} %param.18) | copy-start | bytes 1523716
  7.4 93.4 %all-gather.3.cloned.1.call-start = ((), (), s32[]{:S(2)}) async-start(), calls=%async_computation.2 | async-start | bytes 2129920 | tf_op jit(solution)/shard_map/all_gather | solution.py:93
  8.5 1.2 copy-start.8
  11.4 5.6 %copy-start.18 = (s32[1,1,128]{2,1,0:T(1,128)S(1)}, s32[1,1,128]{2,1,0:T(1,128)}, u32[]{:S(2)}) copy-start(s32[1,1,128]{2,1,0:T(1,128)} %param.19) | copy-start | bytes 1540
  20.2 15.4 %copy-start.10 = (bf16[1024,64]{0,1:T(8,128)(2,1)S(1)}, bf16[1024,64]{0,1:T(8,128)(2,1)}, u32[]{:S(2)}) copy-start(bf16[1024,64]{0,1:T(8,128)(2,1)} %param.12) | copy-start | bytes 393220
  20.2 15.4 %copy-start.14 = (bf16[1024,64]{0,1:T(8,128)(2,1)S(1)}, bf16[1024,64]{0,1:T(8,128)(2,1)}, u32[]{:S(2)}) copy-start(bf16[1024,64]{0,1:T(8,128)(2,1)} %param.13) | copy-start | bytes 393220
  20.2 21.1 %copy-start.17 = (s32[256]{0:T(256)S(1)}, s32[256]{0:T(256)}, u32[]{:S(2)}) copy-start(s32[256]{0:T(256)} %param.21) | copy-start | bytes 3076
  20.2 21.2 %copy-start.16 = (s32[256]{0:T(256)S(1)}, s32[256]{0:T(256)}, u32[]{:S(2)}) copy-start(s32[256]{0:T(256)} %param.20) | copy-start | bytes 3076
  22.3 87.2 %all-to-all-start = ((bf16[64,2,4096]{2,1,0:T(2,128)(2,1)}), bf16[64,2,4096]{2,1,0:T(2,128)(2,1)}, u32[]{:S(2)}, u32[]{:S(2)}) async-start(bf16[64,2,4096]{2,1,0:T(2,128)(2,1)} %broadcast_select_fusion), calls=%async_computation | async-start | bytes 2097152 | tf_op jit(solution)/shard_map/all_to_all | solution.py:115
  35.5 163.9 %all-reduce.2.cloned.1.call-start = ((), (), s32[]{:S(2)}) async-start(), calls=%async_computation.1 | async-start | bytes 1048576 | tf_op jit(solution)/shard_map/psum | solution.py:136
  35.7 21.6 %collective-permute-start = (bf16[64,128]{0,1:T(8,128)(2,1)S(1)}, bf16[64,128]{0,1:T(8,128)(2,1)S(1)}, u32[]{:S(2)}, u32[]{:S(2)}) collective-permute-start(bf16[64,128]{0,1:T(8,128)(2,1)S(1)} %get-tuple-element.18), channel_id=1, source_target_pairs={{0,4},{4,8},{8,12},{12,16},{16,20},{20,24},{24,28},{28,32},{32,36}... | collective-permute-start | bytes 49160 | tf_op jit(solution)/shard_map/ppermute | solution.py:25
  39.3 22.5 %collective-permute-start.1 = (bf16[64,128]{0,1:T(8,128)(2,1)S(1)}, bf16[64,128]{0,1:T(8,128)(2,1)S(1)}, u32[]{:S(2)}, u32[]{:S(2)}) collective-permute-start(bf16[64,128]{0,1:T(8,128)(2,1)S(1)} %get-tuple-element.17), channel_id=1, source_target_pairs={{4,0},{8,4},{12,8},{16,12},{20,16},{24,20},{28,24},{32,28},{36,32}... | collective-permute-start | bytes 49160 | tf_op jit(solution)/shard_map/ppermute | solution.py:26
  105.4 1.2 copy-start.9
  106.6 1.0 copy-start.3
  107.6 0.8 copy-start.5
  130.2 2.2 %copy-start.1 = (f32[128,64,64]{0,2,1:T(8,128)S(1)}, f32[128,64,64]{0,2,1:T(8,128)}, u32[]{:S(2)}) copy-start(f32[128,64,64]{0,2,1:T(8,128)} %copy.77) | copy-start | bytes 6291460
  137.5 5.6 %copy-start.2 = (bf16[128,64,64]{2,1,0:T(8,128)(2,1)S(1)}, bf16[128,64,64]{2,1,0:T(8,128)(2,1)}, u32[]{:S(2)}) copy-start(bf16[128,64,64]{2,1,0:T(8,128)(2,1)} %copy.105) | copy-start | bytes 3145732
  152.6 1.2 copy-start.4
  152.6 1.3 copy-start.6
  154.4 2.0 copy-start.12
  154.4 2.0 copy-start.13
  156.1 47.9 %copy-start.7 = (bf16[31,64,64]{2,1,0:T(8,128)(2,1)S(1)}, bf16[31,64,64]{2,1,0:T(8,128)(2,1)}, u32[]{:S(2)}) copy-start(bf16[31,64,64]{2,1,0:T(8,128)(2,1)} %param.15) | copy-start | bytes 761860
  204.2 1.4 copy-start.11
  205.1 1.0 copy-start.15
Sparse Core Ops, SparseCore 0:
  16.5 84.1 all-gather.2
Sparse Core Ops, SparseCore 1:
  156.2 43.1 all-reduce.1
where the time goes:
time: 218 us; the launch traced here: 215 us
  waiting for transfers between devices  84.8 us (39%)
  local copies, waits for them, and re-layouts  56.6 us (26%)
  matrix products  31.3 us (14%)
  starting transfers between devices  18.9 us (9%)
  between operations  15.7 us (7%)
  other arithmetic  8.11 us (4%)
    psum x1, waiting for transfers between devices, body(): summed = lax.psum(partial_value, 'cpl').reshape(box_count, RANK, NRHS)  37.3 us
    all_gather x1, waiting for transfers between devices, body(): raised = lax.all_gather(root_up[None], 'leaf', axis=0, tiled=True)  36.4 us
    unnamed x46, local copies, waits for them, and re-layouts  14.5 us
    all_to_all x1, starting transfers between devices, body(): lax.all_to_all(outgoing_rows, 'leaf', split_axis=0, concat_axis=0, tiled=...  13.2 us
    dot_general x2, matrix products, body(): jnp.einsum('brs,bsn->brn', matrices, sources, preferred_element_type=jnp....  10.3 us
    reshape x2, local copies, waits for them, and re-layouts, body(): jnp.take(received, block_slot[offset:offset + block_rows], axis=0)  9.99 us
    dot_general x2, local copies, waits for them, and re-layouts, body(): jnp.einsum('brs,bsn->brn', matrices, sources, preferred_element_type=jnp....  9.81 us
    dot_general x14, matrix products, push_down(): jnp.einsum('brs,bsn->brn', matrices.astype(jnp.float32), fields, precisio...  7.37 us
  transfers between devices with their start and end apart: 5, of which 4 were waited for; matrix products, arithmetic and copies ran while one was open for 14% of the time, Pallas kernels for 0%

commit v1 on v0

v1 whole, which is shorter than its diff:
```python
import functools

import jax
import jax.numpy as jnp
from jax import lax
from jax.experimental import pallas as pl
from jax.experimental.pallas import tpu as pltpu
from jax.sharding import PartitionSpec as P

RANK = 64
NRHS = 64
LEAF = 64
B_DEV = 16
BOX = 2 * B_DEV - 1
BLK = 256
SHARE = 4
POS = 288
STEPS = POS // 2
PACK = 5

MESH = pl.DeviceIdType.MESH
f32, bf16, i32 = jnp.float32, jnp.bfloat16, jnp.int32
sqrt_three = 1.7320508075688772


def nn(a, b):
    return lax.dot_general(a, b, (((1,), (0,)), ((), ())), preferred_element_type=f32)


def nt(a, b):
    return lax.dot_general(a, b, (((1,), (1,)), ((), ())), preferred_element_type=f32)


def split_rows(x):
    upper = x.astype(bf16)
    lower = (x - upper.astype(f32)).astype(bf16)
    return jnp.concatenate([upper, lower], axis=0)


def wide(dot, x, w):
    rows = x.shape[0]
    y = dot(split_rows(x), w)
    return y[:rows] + y[rows:]


def lane_of(shape):
    return lax.broadcasted_iota(i32, shape, 1)


def row_of(shape):
    return lax.broadcasted_iota(i32, shape, 0)


def spread(tile):
    left = lane_of(tile.shape) < 64
    none = jnp.zeros_like(tile)
    return jnp.concatenate([jnp.where(left, tile, none), jnp.where(left, none, tile)], axis=0)


def kernel(
    n_leaf,
    vec_h, emb_h, bas_h, tra_h, cou_h, ttr_h, tco_h, send_boxes, slot_ref, target_ref,
    out_ref,
    vec, emb, bas, tra, cou, ttr, tco,
    left_box, right_box, outgoing, incoming, root_dup,
    top_out, top_in, top_coef, top_share, top_all,
    index_v, start_v, index_s, start_s,
    rows_f, blocks, prefix, field_f, field_b, field_in, near_ref,
    local_sem, halo_send, halo_recv, a2a_send, a2a_recv, top_send, top_recv,
    field_send, field_recv, down_send, down_recv,
):
    height = n_leaf.bit_length() - 1
    me = lax.axis_index("leaf")
    col = lax.axis_index("cpl")

    def peer(step):
        return lax.rem(me + step, n_leaf)

    def other(step):
        return lax.rem(col + step, SHARE)

    barrier = pltpu.get_barrier_semaphore()

    def greet(step, carry):
        pl.semaphore_signal(barrier, inc=1, device_id=(peer(step), col), device_id_type=MESH)
        return carry

    lax.fori_loop(1, n_leaf, greet, 0)
    for step in range(1, SHARE):
        pl.semaphore_signal(barrier, inc=1, device_id=(me, other(step)), device_id_type=MESH)

    loads = [
        pltpu.make_async_copy(vec_h, vec.at[:, pl.ds(128, 1024)], local_sem.at[0]),
        pltpu.make_async_copy(bas_h, bas, local_sem.at[1]),
        pltpu.make_async_copy(tra_h, tra, local_sem.at[2]),
        pltpu.make_async_copy(emb_h, emb.at[:, pl.ds(128, 1024)], local_sem.at[3]),
        pltpu.make_async_copy(cou_h, cou, local_sem.at[4]),
        pltpu.make_async_copy(ttr_h, ttr, local_sem.at[5]),
        pltpu.make_async_copy(tco_h, tco, local_sem.at[6]),
    ]
    for load in loads:
        load.start()

    loads[0].wait()
    loads[1].wait()
    tiles = []
    for j in range(B_DEV // 2):
        v = vec[:, 128 * (j + 1) : 128 * (j + 2)]
        tiles.append(nt(v, spread(bas[:, 128 * j : 128 * (j + 1)])))

    def keep_pair(first, tile):
        rounded = tile.astype(bf16)
        turned = pltpu.roll(rounded, 64, 1)
        left_box[first] = rounded
        right_box[first] = turned
        left_box[first + 1] = turned
        right_box[first + 1] = rounded

    loads[2].wait()
    first = B_DEV - 1
    for j, tile in enumerate(tiles):
        keep_pair(first + 2 * j, tile)
    while len(tiles) > 1:
        raised = []
        for j in range(len(tiles) // 2):
            w = tra[first + 4 * j : first + 4 * j + 4].reshape(256, 64)
            w = jnp.concatenate([w, w], axis=1)
            w = jnp.where((row_of(w.shape) < 128) == (lane_of(w.shape) < 64), w, jnp.zeros_like(w))
            raised.append(wide(nn, jnp.concatenate(tiles[2 * j : 2 * j + 2], axis=1), w))
        first = (first - 1) // 2
        tiles = raised
        for j, tile in enumerate(tiles):
            keep_pair(first + 2 * j, tile)
    w = tra[1:3].reshape(128, 64)
    root = wide(nn, tiles[0], jnp.concatenate([w, w], axis=1))
    left_box[0] = root.astype(bf16)
    right_box[0] = root.astype(bf16)

    pl.semaphore_wait(barrier, n_leaf - 1 + SHARE - 1)

    half = lane_of((64, 128)) < 64

    def a2a_copy(step):
        return pltpu.make_async_remote_copy(
            src_ref=outgoing.at[step],
            dst_ref=incoming.at[me],
            send_sem=a2a_send.at[step],
            recv_sem=a2a_recv.at[me],
            device_id=(peer(step), col),
            device_id_type=MESH,
        )

    def pick(d):
        return jnp.where(
            half, left_box[send_boxes[0, 0, 2 * d]], right_box[send_boxes[0, 0, 2 * d + 1]]
        )

    def give(i, carry):
        step = lax.rem((i // 2 + 1) * (1 - 2 * lax.rem(i, 2)) + n_leaf, n_leaf)
        outgoing[step] = pick(peer(step))
        a2a_copy(step).start()
        return carry

    lax.fori_loop(0, n_leaf - 1, give, 0)
    incoming[me] = pick(me)

    halos = []
    for k, (src_h, dst) in enumerate(((vec_h, vec), (emb_h, emb))):
        for side, (lanes, to, at) in enumerate(
            ((pl.ds(896, 128), peer(1), 0), (pl.ds(0, 128), peer(n_leaf - 1), 1152))
        ):
            halos.append(
                pltpu.make_async_remote_copy(
                    src_ref=src_h.at[:, lanes],
                    dst_ref=dst.at[:, pl.ds(at, 128)],
                    send_sem=halo_send.at[2 * k + side],
                    recv_sem=halo_recv.at[2 * k + side],
                    device_id=(to, col),
                    device_id_type=MESH,
                )
            )
            halos[-1].start()

    w = tra[0]
    root_dup[...] = wide(nn, root[:, :64], jnp.concatenate([w, w], axis=1))
    quarter = pl.multiple_of(col * 16, 16)
    half8 = lane_of((8, 128)) < 64
    top_out[...] = jnp.where(
        half8, root_dup[pl.ds(quarter, 8), :], root_dup[pl.ds(pl.multiple_of(quarter + 8, 8), 8), :]
    )

    def top_copy(step):
        return pltpu.make_async_remote_copy(
            src_ref=top_out,
            dst_ref=top_in.at[me],
            send_sem=top_send.at[step],
            recv_sem=top_recv.at[me],
            device_id=(peer(step), col),
            device_id_type=MESH,
        )

    def give_top(i, carry):
        step = lax.rem((i // 2 + 1) * (1 - 2 * lax.rem(i, 2)) + n_leaf, n_leaf)
        top_copy(step).start()
        return carry

    lax.fori_loop(0, n_leaf - 1, give_top, 0)
    top_in[me] = top_out[...]

    target = target_ref[...]
    slot = slot_ref[...]
    member = (target == row_of((32, BLK))).astype(f32)
    before = (row_of((BLK, BLK)) < lane_of((BLK, BLK))).astype(bf16)
    earlier = nn(member.astype(bf16), before)
    count = jnp.sum(member, axis=1, keepdims=True).astype(i32)
    even = ((count + 1) // 2) * 2
    even = jnp.where(row_of((32, 1)) < BOX, even, 0)
    below = (lane_of((32, 32)) < row_of((32, 32))).astype(bf16)
    start = nn(below, jnp.broadcast_to(even.astype(f32), (32, 128)).astype(bf16))
    start_v[...] = (start * 0.5).astype(i32)
    base = jnp.where(row_of((32, 1)) < BOX, start[:, :1], 4.0 * POS)
    rank = jnp.sum(member * (earlier + base), axis=0, keepdims=True).astype(i32)
    chosen = rank == row_of((POS, BLK))
    chosen_b = chosen.astype(bf16)
    pair_row = jnp.broadcast_to((slot // 2).astype(f32), (16, BLK)).astype(bf16)
    index_v[...] = nt(pair_row, chosen_b)[:8].astype(i32)
    odd = (slot - (slot // 2) * 2).astype(f32)
    odd_col = jnp.sum(jnp.where(chosen, odd, 0.0), axis=1, keepdims=True)
    half_f = (lane_of((POS, 128)) >= 64).astype(f32)
    used_half = (half_f == odd_col).astype(f32)
    copies = [
        pltpu.make_async_copy(index_v, index_s, local_sem.at[7]),
        pltpu.make_async_copy(start_v, start_s, local_sem.at[8]),
    ]
    for copy in copies:
        copy.start()

    loads[4].wait()

    def turn(r, carry):
        x, y = cou[r], cou[r + 32]
        d = nt(chosen_b, jnp.concatenate([x, x, y, y], axis=0))
        rows_f[pl.ds(r, POS, stride=64), :] = d[:, :128] * used_half
        rows_f[pl.ds(r + 32, POS, stride=64), :] = d[:, 128:] * used_half
        return carry

    lax.fori_loop(0, 32, turn, 0)

    def narrow(j, carry):
        blocks[j] = rows_f[pl.ds(pl.multiple_of(j * 64, 64), 64), :].astype(bf16)
        return carry

    lax.fori_loop(0, POS, narrow, 0)
    for copy in copies:
        copy.wait()

    loads[3].wait()
    for halo in halos:
        halo.wait()
    window = pl.ds(pl.multiple_of(col * 256, 256), 512)
    emb_t = emb[:, window]
    vec_t = vec[:, window]
    emb_w = emb_t.T
    squares = emb_w.astype(f32) * emb_w.astype(f32)
    norm_w = jnp.sum(squares, axis=1, keepdims=True)
    for a in range(2):
        own = emb_t[:, 128 * (a + 1) : 128 * (a + 2)]
        own_f = own.astype(f32)
        own_norm = jnp.sum(own_f * own_f, axis=0, keepdims=True)
        lo = 128 * a + 64
        inner = nn(emb_w[lo : lo + 256], own)
        distance = jnp.sqrt(jnp.maximum(norm_w[lo : lo + 256] + own_norm - 2.0 * inner, 0.0))
        scaled = sqrt_three * distance
        value = (1.0 + scaled) * jnp.exp(-scaled)
        row, lane = row_of((256, 128)), lane_of((256, 128))
        gap = row // 64 - lane // 64
        live = (gap >= 0) & (gap <= 2)
        if a == 0:
            live = live & ((row >= 64) | (me + col > 0))
        else:
            live = live & ((row < 192) | (me * SHARE + col < n_leaf * SHARE - 1))
        value = jnp.where(live, value, 0.0).astype(bf16)
        blank = jnp.zeros((64, 128), bf16)
        value = jnp.concatenate([blank, value, blank], axis=0)
        near_ref[:, 128 * a : 128 * (a + 1)] = nn(vec_t[:, 128 * a : 128 * a + 384], value)

    def arrived(step, carry):
        source = peer(step)
        pltpu.make_async_remote_copy(
            src_ref=outgoing.at[step],
            dst_ref=incoming.at[source],
            send_sem=a2a_send.at[step],
            recv_sem=a2a_recv.at[source],
            device_id=(source, col),
            device_id_type=MESH,
        ).wait()
        return carry

    lax.fori_loop(1, n_leaf, arrived, 0)

    prefix[0] = jnp.zeros((64, 64), f32)

    def from_pair(j):
        return jnp.clip(index_s[0, j], 0, n_leaf - 1)

    def couple(u, acc):
        source = jnp.concatenate(
            [incoming[from_pair(2 * u)], incoming[from_pair(2 * u + 1)]], axis=1
        )
        matrix = jnp.concatenate([blocks[2 * u], blocks[2 * u + 1]], axis=1)
        acc = acc + nt(source, matrix)
        prefix[u + 1] = acc
        return acc

    lax.fori_loop(0, STEPS, couple, jnp.zeros((64, 64), f32), unroll=4)

    def run(m):
        return jnp.clip(start_s[m, 0], 0, STEPS)

    def field(m):
        return prefix[run(m + 1)] - prefix[run(m)]

    def pair(a, b):
        return jnp.concatenate([field(a), field(b)], axis=1)

    for q in range(SHARE):
        packed = (
            pair(15 + 4 * q, 16 + 4 * q),
            pair(17 + 4 * q, 18 + 4 * q),
            pair(7 + 2 * q, 8 + 2 * q),
            pair(3 + q, 1 + q // 2),
            pair(0, 0),
        )
        for i, tile in enumerate(packed):
            field_f[q, i] = tile
            field_b[q, i] = tile.astype(bf16)

    def field_copy(step):
        return pltpu.make_async_remote_copy(
            src_ref=field_b.at[other(step)],
            dst_ref=field_in.at[col],
            send_sem=field_send.at[step],
            recv_sem=field_recv.at[col],
            device_id=(me, other(step)),
            device_id_type=MESH,
        )

    for step in range(1, SHARE):
        field_copy(step).start()

    loads[5].wait()
    loads[6].wait()

    def top_arrived(step, carry):
        source = peer(step)
        pltpu.make_async_remote_copy(
            src_ref=top_out,
            dst_ref=top_in.at[source],
            send_sem=top_send.at[step],
            recv_sem=top_recv.at[source],
            device_id=(source, col),
            device_id_type=MESH,
        ).wait()
        return carry

    lax.fori_loop(1, n_leaf, top_arrived, 0)
    for k in range(n_leaf // 2):
        both = top_in[2 * k] + top_in[2 * k + 1]
        top_coef[n_leaf // 2 + k] = jnp.concatenate([both[:, :64], both[:, 64:]], axis=0)
    for level in range(height - 2, 0, -1):
        for k in range(1 << level, 2 << level):
            children = jnp.concatenate([top_coef[2 * k], top_coef[2 * k + 1]], axis=1)
            top_coef[k] = wide(nn, children, ttr[2 * k - 2 : 2 * k].reshape(128, 64))
    down = None
    for level in range(1, height):
        node = (n_leaf + me) // (1 << (height - level))
        sibling = node + 1 - 2 * lax.rem(node, 2)
        here = wide(nt, top_coef[sibling], tco[node - 2])
        down = here if down is None else here + wide(nt, down, ttr[node - 2])
    top_share[...] = jnp.concatenate([down[:8], down[8:]], axis=1)

    def down_copy(step):
        return pltpu.make_async_remote_copy(
            src_ref=top_share,
            dst_ref=top_all.at[col],
            send_sem=down_send.at[step],
            recv_sem=down_recv.at[col],
            device_id=(me, other(step)),
            device_id_type=MESH,
        )

    for step in range(1, SHARE):
        down_copy(step).start()
    top_all[col] = top_share[...]

    def down_arrived(step):
        source = other(step)
        pltpu.make_async_remote_copy(
            src_ref=top_share,
            dst_ref=top_all.at[source],
            send_sem=down_send.at[step],
            recv_sem=down_recv.at[source],
            device_id=(me, source),
            device_id_type=MESH,
        ).wait()

    def field_arrived(step):
        source = other(step)
        pltpu.make_async_remote_copy(
            src_ref=field_b.at[source],
            dst_ref=field_in.at[source],
            send_sem=field_send.at[step],
            recv_sem=field_recv.at[source],
            device_id=(me, source),
            device_id_type=MESH,
        ).wait()

    for step in range(1, SHARE):
        field_arrived(step)
        down_arrived(step)

    def total(i):
        value = field_f[col, i]
        for step in range(1, SHARE):
            value = value + field_in[other(step), i].astype(f32)
        return value

    pieces = []
    for q in range(SHARE):
        tile = top_all[q]
        pieces += [tile[:, :64], tile[:, 64:]]
    parent = jnp.concatenate(pieces, axis=0)
    upper = total(3)
    down0 = total(4)[:, :64] + wide(nt, parent, tra[0])
    down1 = upper[:, 64:] + wide(nt, down0, tra[1 + col // 2])
    down2 = upper[:, :64] + wide(nt, down1, tra[3 + col])
    down3 = total(2) + wide(nt, down2, tra[pl.ds(7 + 2 * col, 2)].reshape(128, 64))
    for a in range(2):
        w = tra[pl.ds(15 + 4 * col + 2 * a, 2)].reshape(128, 64)
        leaf = total(a) + wide(nt, down3[:, 64 * a : 64 * (a + 1)], w)
        b = bas[:, pl.ds(pl.multiple_of(col * 256 + 128 * a, 128), 128)]
        out_ref[:, 128 * a : 128 * (a + 1)] = near_ref[:, 128 * a : 128 * (a + 1)] + nn(
            leaf.astype(bf16), spread(b)
        )


def body(
    vectors, embeddings, basis, transfer, coupling, top_transfer, top_coupling,
    send_boxes, block_slot, block_target,
):
    n_leaf = lax.axis_size("leaf")
    tops = top_transfer.shape[0]
    hbm = pl.BlockSpec(memory_space=pl.ANY)
    vmem = pl.BlockSpec(memory_space=pltpu.VMEM)
    smem = pl.BlockSpec(memory_space=pltpu.SMEM)
    dma = pltpu.SemaphoreType.DMA
    result = pl.pallas_call(
        functools.partial(kernel, n_leaf),
        out_shape=jax.ShapeDtypeStruct((NRHS, SHARE * LEAF), f32),
        in_specs=[hbm] * 7 + [smem, vmem, vmem],
        out_specs=vmem,
        scratch_shapes=[
            pltpu.VMEM((64, 1280), bf16),
            pltpu.VMEM((64, 1280), bf16),
            pltpu.VMEM((64, 1024), bf16),
            pltpu.VMEM((BOX, 64, 64), bf16),
            pltpu.VMEM((64, 64, BLK), bf16),
            pltpu.VMEM((tops, 64, 64), bf16),
            pltpu.VMEM((tops, 64, 64), bf16),
            pltpu.VMEM((BOX, 64, 128), bf16),
            pltpu.VMEM((BOX, 64, 128), bf16),
            pltpu.VMEM((n_leaf, 64, 128), bf16),
            pltpu.VMEM((n_leaf, 64, 128), bf16),
            pltpu.VMEM((64, 128), f32),
            pltpu.VMEM((8, 128), f32),
            pltpu.VMEM((n_leaf, 8, 128), f32),
            pltpu.VMEM((n_leaf, 16, 64), f32),
            pltpu.VMEM((8, 128), f32),
            pltpu.VMEM((SHARE, 8, 128), f32),
            pltpu.VMEM((8, POS), i32),
            pltpu.VMEM((32, 128), i32),
            pltpu.SMEM((8, POS), i32),
            pltpu.SMEM((32, 128), i32),
            pltpu.VMEM((POS * 64 + 64, 128), f32),
            pltpu.VMEM((POS, 64, 128), bf16),
            pltpu.VMEM((STEPS + 1, 64, 64), f32),
            pltpu.VMEM((SHARE, PACK, 64, 128), f32),
            pltpu.VMEM((SHARE, PACK, 64, 128), bf16),
            pltpu.VMEM((SHARE, PACK, 64, 128), bf16),
            pltpu.VMEM((64, SHARE * LEAF), f32),
            dma((9,)),
            dma((4,)),
            dma((4,)),
            dma((n_leaf,)),
            dma((n_leaf,)),
            dma((n_leaf,)),
            dma((n_leaf,)),
            dma((SHARE,)),
            dma((SHARE,)),
            dma((SHARE,)),
            dma((SHARE,)),
        ],
        compiler_params=pltpu.CompilerParams(
            collective_id=0, has_side_effects=True, vmem_limit_bytes=56 * 1024 * 1024
        ),
    )(
        vectors.T, embeddings.T, basis.T, transfer, jnp.transpose(coupling, (1, 2, 0)),
        top_transfer, top_coupling, send_boxes,
        block_slot.reshape(1, BLK), block_target.reshape(1, BLK),
    )
    return result.T


def solution(mesh):
    placed = (
        P("leaf", None),
        P("leaf", None),
        P("leaf", None),
        P("leaf", None, None),
        P(("leaf", "cpl"), None, None),
        P(),
        P(),
        P("leaf", "cpl", None),
        P(("leaf", "cpl")),
        P(("leaf", "cpl")),
    )
    return jax.shard_map(
        body, mesh=mesh, in_specs=placed, out_specs=P(("leaf", "cpl"), None), check_vma=False
    )
```

time: 218 us -> 59.3 us (0.27); the launches traced: 215 us -> 59.2 us
  waiting for transfers between devices: 84.8 us -> 0 us
  Pallas kernels: 0 us -> 57.7 us
  local copies, waits for them, and re-layouts: 56.6 us -> 1.47 us
  matrix products: 31.3 us -> 0 us
  starting transfers between devices: 18.9 us -> 0 us
  between operations: 15.7 us -> 0.01 us
  other arithmetic: 8.11 us -> 0 us
    pallas_call x0 -> x1, Pallas kernels: none -> 57.7 us  [body(): pl.pallas_call(functools.partial(kernel, n_leaf), out_shape=jax.ShapeDtyp...]
    psum x1 -> x0, waiting for transfers between devices: 37.3 us -> none  [body(): summed = lax.psum(partial_value, 'cpl').reshape(box_count, RANK, NRHS)]
    all_gather x1 -> x0, waiting for transfers between devices: 36.4 us -> none  [body(): raised = lax.all_gather(root_up[None], 'leaf', axis=0, tiled=True)]
    dot_general x34 -> x0, matrix products: 31.3 us -> none  [the longest x2 10.3 us: body(): jnp.einsum('brs,bsn->brn', matrices, sources, preferred_element_type=jnp....]
    all_to_all x1 -> x0, starting transfers between devices: 13.2 us -> none  [body(): lax.all_to_all(outgoing_rows, 'leaf', split_axis=0, concat_axis=0, tiled=...]
    unnamed x46 -> x1, local copies, waits for them, and re-layouts: 14.5 us -> 1.47 us
    reshape x5 -> x0, local copies, waits for them, and re-layouts: 12 us -> none  [the longest x2 9.99 us: body(): jnp.take(received, block_slot[offset:offset + block_rows], axis=0)]
    ppermute x2 -> x0, waiting for transfers between devices: 11 us -> none  [the longest x1 6.59 us: with_halo(): before = lax.ppermute(last, axis, up)]
  transfers between devices with their start and end apart: 5 -> 0, of which waited for: 4 -> 0; matrix products, arithmetic and copies ran while one was open for 14% -> 0% of each run, Pallas kernels for 0% -> 0%
where the time goes in v1:
time: 59.3 us; the launch traced here: 59.2 us
  Pallas kernels  57.7 us (97%)
  local copies, waits for them, and re-layouts  1.47 us (2%)
    pallas_call x1, Pallas kernels, body(): pl.pallas_call(functools.partial(kernel, n_leaf), out_shape=jax.ShapeDtyp...  57.7 us
    unnamed x1, local copies, waits for them, and re-layouts  1.47 us

profile of v1, /device:TPU:1, one launch (start us, length us, event | category | flops | bytes accessed | tf_op | source)
XLA Modules:
  0.0 59.2 jit_solution(16307392765583660938)
XLA Ops:
  0.0 57.7 %shard_map.100 = f32[64,256]{1,0:T(8,128)} custom-call(bf16[64,1024]{1,0:T(8,128)(2,1)} %bitcast.9, bf16[64,1024]{1,0:T(8,128)(2,1)} %bitcast.10, bf16[64,1024]{1,0:T(8,128)(2,1)} %bitcast.11, bf16[31,64,64]{2,1,0:T(8,128)(2,1)} %tra_h.1, bf16[64,64,256]{2,1,0:T(8,128)(2,1)} %bitcast.7, bf16[62,64,64]{2,1,0:T(8,128)(2,1)} %ttr_h.1, ...), custom_call_target="tpu_custom_call" | custom-call | tf_op jit(solution)/shard_map/pallas_call | solution.py:457
  57.7 1.5 %copy.12 = f32[256,64]{0,1:T(8,128)} copy(f32[256,64]{0,1:T(8,128)} %bitcast.8) | data formatting | bytes 131072

commit v2 on v1

--- a/solution.py
+++ b/solution.py
@@ -16,7 +16,7 @@
 SHARE = 4
 POS = 288
 STEPS = POS // 2
-PACK = 5
+GROUP = 16
 
 MESH = pl.DeviceIdType.MESH
 f32, bf16, i32 = jnp.float32, jnp.bfloat16, jnp.int32
@@ -63,11 +63,11 @@
     out_ref,
     vec, emb, bas, tra, cou, ttr, tco,
     left_box, right_box, outgoing, incoming, root_dup,
-    top_out, top_in, top_coef, top_share, top_all,
+    lifts, top_out, top_in, group_coef, group_out, group_in, upper_coef, top_share, top_all,
     index_v, start_v, index_s, start_s,
-    rows_f, blocks, prefix, field_f, field_b, field_in, near_ref,
+    rows_f, blocks, prefix, leaf_f, leaf_b, leaf_in, near_ref,
     local_sem, halo_send, halo_recv, a2a_send, a2a_recv, top_send, top_recv,
-    field_send, field_recv, down_send, down_recv,
+    group_send, group_recv, field_send, field_recv, down_send, down_recv,
 ):
     height = n_leaf.bit_length() - 1
     me = lax.axis_index("leaf")
@@ -126,6 +126,7 @@
             w = tra[first + 4 * j : first + 4 * j + 4].reshape(256, 64)
             w = jnp.concatenate([w, w], axis=1)
             w = jnp.where((row_of(w.shape) < 128) == (lane_of(w.shape) < 64), w, jnp.zeros_like(w))
+            lifts[len(tiles) // 2 - 1 + j] = w
             raised.append(wide(nn, jnp.concatenate(tiles[2 * j : 2 * j + 2], axis=1), w))
         first = (first - 1) // 2
         tiles = raised
@@ -137,6 +138,44 @@
     right_box[0] = root.astype(bf16)
 
     pl.semaphore_wait(barrier, n_leaf - 1 + SHARE - 1)
+
+    group = me // GROUP
+    groups = n_leaf // GROUP
+    inside = lax.rem(me, GROUP)
+    w = tra[0]
+    root_dup[...] = wide(nn, root[:, :64], jnp.concatenate([w, w], axis=1))
+    quarter = pl.multiple_of(col * 16, 16)
+    half8 = lane_of((8, 128)) < 64
+    top_out[...] = jnp.where(
+        half8, root_dup[pl.ds(quarter, 8), :], root_dup[pl.ds(pl.multiple_of(quarter + 8, 8), 8), :]
+    )
+
+    def mate(step):
+        return lax.rem(inside + step, GROUP)
+
+    def top_copy(step, source):
+        return pltpu.make_async_remote_copy(
+            src_ref=top_out,
+            dst_ref=top_in.at[source],
+            send_sem=top_send.at[step],
+            recv_sem=top_recv.at[source],
+            device_id=(group * GROUP + mate(step), col),
+            device_id_type=MESH,
+        )
+
+    def group_copy(step, source):
+        return pltpu.make_async_remote_copy(
+            src_ref=group_out,
+            dst_ref=group_in.at[source],
+            send_sem=group_send.at[step],
+            recv_sem=group_recv.at[source],
+            device_id=(lax.rem(group + step, groups) * GROUP + inside, col),
+            device_id_type=MESH,
+        )
+
+    for step in range(1, GROUP):
+        top_copy(step, inside).start()
+    top_in[inside] = top_out[...]
 
     half = lane_of((64, 128)) < 64
 
@@ -180,32 +219,6 @@
                 )
             )
             halos[-1].start()
-
-    w = tra[0]
-    root_dup[...] = wide(nn, root[:, :64], jnp.concatenate([w, w], axis=1))
-    quarter = pl.multiple_of(col * 16, 16)
-    half8 = lane_of((8, 128)) < 64
-    top_out[...] = jnp.where(
-        half8, root_dup[pl.ds(quarter, 8), :], root_dup[pl.ds(pl.multiple_of(quarter + 8, 8), 8), :]
-    )
-
-    def top_copy(step):
-        return pltpu.make_async_remote_copy(
-            src_ref=top_out,
-            dst_ref=top_in.at[me],
-            send_sem=top_send.at[step],
-            recv_sem=top_recv.at[me],
-            device_id=(peer(step), col),
-            device_id_type=MESH,
-        )
-
-    def give_top(i, carry):
-        step = lax.rem((i // 2 + 1) * (1 - 2 * lax.rem(i, 2)) + n_leaf, n_leaf)
-        top_copy(step).start()
-        return carry
-
-    lax.fori_loop(0, n_leaf - 1, give_top, 0)
-    top_in[me] = top_out[...]
 
     target = target_ref[...]
     slot = slot_ref[...]
@@ -235,6 +248,30 @@
     for copy in copies:
         copy.start()
 
+    def unpack(tile):
+        return jnp.concatenate([tile[:, :64], tile[:, 64:]], axis=0)
+
+    def pack(value):
+        return jnp.concatenate([value[:8], value[8:]], axis=1)
+
+    loads[5].wait()
+    loads[6].wait()
+    for step in range(1, GROUP):
+        top_copy(step, mate(step)).wait()
+    depth = GROUP.bit_length() - 1
+    for k in range(GROUP // 2):
+        group_coef[GROUP // 2 + k] = unpack(top_in[2 * k] + top_in[2 * k + 1])
+    for level in range(depth - 2, -1, -1):
+        for k in range(1 << level):
+            child = 2 * ((1 << level) + k)
+            children = jnp.concatenate([group_coef[child], group_coef[child + 1]], axis=1)
+            matrix = ttr[pl.ds(((groups + group) << (level + 1)) + 2 * k - 2, 2)].reshape(128, 64)
+            group_coef[(1 << level) + k] = wide(nn, children, matrix)
+    group_out[...] = pack(group_coef[1])
+    for step in range(1, groups):
+        group_copy(step, group).start()
+    group_in[group] = group_out[...]
+
     loads[4].wait()
 
     def turn(r, carry):
@@ -244,13 +281,47 @@
         rows_f[pl.ds(r + 32, POS, stride=64), :] = d[:, 128:] * used_half
         return carry
 
-    lax.fori_loop(0, 32, turn, 0)
+    lax.fori_loop(0, 32, turn, 0, unroll=4)
+
+    for step in range(1, groups):
+        group_copy(step, lax.rem(group + step, groups)).wait()
+    for k in range(groups):
+        upper_coef[groups + k] = unpack(group_in[k])
+    for k in range(groups - 1, 1, -1):
+        children = jnp.concatenate([upper_coef[2 * k], upper_coef[2 * k + 1]], axis=1)
+        upper_coef[k] = wide(nn, children, ttr[2 * k - 2 : 2 * k].reshape(128, 64))
+    down = None
+    for level in range(1, height):
+        node = (n_leaf + me) // (1 << (height - level))
+        sibling = node + 1 - 2 * lax.rem(node, 2)
+        below = level - (groups.bit_length() - 1)
+        if below <= 0:
+            beside = upper_coef[sibling]
+        else:
+            beside = group_coef[sibling - ((groups + group) << below) + (1 << below)]
+        here = wide(nt, beside, tco[node - 2])
+        down = here if down is None else here + wide(nt, down, ttr[node - 2])
+    top_share[...] = pack(down)
+
+    def down_copy(step, source):
+        return pltpu.make_async_remote_copy(
+            src_ref=top_share,
+            dst_ref=top_all.at[source],
+            send_sem=down_send.at[step],
+            recv_sem=down_recv.at[source],
+            device_id=(me, other(step)),
+            device_id_type=MESH,
+        )
+
+    for step in range(1, SHARE):
+        down_copy(step, col).start()
+    top_all[col] = top_share[...]
 
     def narrow(j, carry):
         blocks[j] = rows_f[pl.ds(pl.multiple_of(j * 64, 64), 64), :].astype(bf16)
         return carry
 
-    lax.fori_loop(0, POS, narrow, 0)
+    lax.fori_loop(0, POS, narrow, 0, unroll=8)
     for copy in copies:
         copy.wait()
 
@@ -284,6 +355,18 @@
         value = jnp.concatenate([blank, value, blank], axis=0)
         near_ref[:, 128 * a : 128 * (a + 1)] = nn(vec_t[:, 128 * a : 128 * a + 384], value)
 
+    for step in range(1, SHARE):
+        down_copy(step, other(step)).wait()
+    parent = jnp.concatenate([unpack(top_all[q]) for q in range(SHARE)], axis=0)
+    parent = wide(nt, parent, tra[0])
+    parent = wide(nt, parent, tra[1 + col // 2])
+    parent = wide(nt, parent, tra[3 + col])
+    parent = wide(nt, parent, tra[pl.ds(7 + 2 * col, 2)].reshape(128, 64))
+    from_top = []
+    for a in range(2):
+        w = tra[pl.ds(15 + 4 * col + 2 * a, 2)].reshape(128, 64)
+        from_top.append(wide(nt, parent[:, 64 * a : 64 * (a + 1)], w))
+
     def arrived(step, carry):
         source = peer(step)
         pltpu.make_async_remote_copy(
@@ -312,7 +395,7 @@
         prefix[u + 1] = acc
         return acc
 
-    lax.fori_loop(0, STEPS, couple, jnp.zeros((64, 64), f32), unroll=4)
+    lax.fori_loop(0, STEPS, couple, jnp.zeros((64, 64), f32), unroll=48)
 
     def run(m):
         return jnp.clip(start_s[m, 0], 0, STEPS)
@@ -323,121 +406,39 @@
     def pair(a, b):
         return jnp.concatenate([field(a), field(b)], axis=1)
 
-    for q in range(SHARE):
-        packed = (
-            pair(15 + 4 * q, 16 + 4 * q),
-            pair(17 + 4 * q, 18 + 4 * q),
-            pair(7 + 2 * q, 8 + 2 * q),
-            pair(3 + q, 1 + q // 2),
-            pair(0, 0),
-        )
-        for i, tile in enumerate(packed):
-            field_f[q, i] = tile
-            field_b[q, i] = tile.astype(bf16)
-
-    def field_copy(step):
+    line = pair(1, 2) + wide(nt, field(0), tra[1:3].reshape(128, 64))
+    lines = [line]
+    for level in range(2, 5):
+        first = (1 << level) - 1
+        lower = []
+        for j, tile in enumerate(lines):
+            both = wide(nt, tile, lifts[len(lines) - 1 + j])
+            lower.append(pair(first + 4 * j, first + 4 * j + 1) + both[:, :128])
+            lower.append(pair(first + 4 * j + 2, first + 4 * j + 3) + both[:, 128:])
+        lines = lower
+    for j, tile in enumerate(lines):
+        leaf_f[j] = tile
+        leaf_b[j] = tile.astype(bf16)
+
+    def field_copy(step, source):
         return pltpu.make_async_remote_copy(
-            src_ref=field_b.at[other(step)],
-            dst_ref=field_in.at[col],
+            src_ref=leaf_b.at[pl.ds(2 * other(step), 2)],
+            dst_ref=leaf_in.at[source],
             send_sem=field_send.at[step],
-            recv_sem=field_recv.at[col],
+            recv_sem=field_recv.at[source],
             device_id=(me, other(step)),
             device_id_type=MESH,
         )
 
     for step in range(1, SHARE):
-        field_copy(step).start()
-
-    loads[5].wait()
-    loads[6].wait()
-
-    def top_arrived(step, carry):
-        source = peer(step)
-        pltpu.make_async_remote_copy(
-            src_ref=top_out,
-            dst_ref=top_in.at[source],
-            send_sem=top_send.at[step],
-            recv_sem=top_recv.at[source],
-            device_id=(source, col),
-            device_id_type=MESH,
-        ).wait()
-        return carry
-
-    lax.fori_loop(1, n_leaf, top_arrived, 0)
-    for k in range(n_leaf // 2):
-        both = top_in[2 * k] + top_in[2 * k + 1]
-        top_coef[n_leaf // 2 + k] = jnp.concatenate([both[:, :64], both[:, 64:]], axis=0)
-    for level in range(height - 2, 0, -1):
-        for k in range(1 << level, 2 << level):
-            children = jnp.concatenate([top_coef[2 * k], top_coef[2 * k + 1]], axis=1)
-            top_coef[k] = wide(nn, children, ttr[2 * k - 2 : 2 * k].reshape(128, 64))
-    down = None
-    for level in range(1, height):
-        node = (n_leaf + me) // (1 << (height - level))
-        sibling = node + 1 - 2 * lax.rem(node, 2)
-        here = wide(nt, top_coef[sibling], tco[node - 2])
-        down = here if down is None else here + wide(nt, down, ttr[node - 2])
-    top_share[...] = jnp.concatenate([down[:8], down[8:]], axis=1)
-
-    def down_copy(step):
-        return pltpu.make_async_remote_copy(
-            src_ref=top_share,
-            dst_ref=top_all.at[col],
-            send_sem=down_send.at[step],
-            recv_sem=down_recv.at[col],
-            device_id=(me, other(step)),
-            device_id_type=MESH,
-        )
-
+        field_copy(step, col).start()
     for step in range(1, SHARE):
-        down_copy(step).start()
-    top_all[col] = top_share[...]
-
-    def down_arrived(step):
-        source = other(step)
-        pltpu.make_async_remote_copy(
-            src_ref=top_share,
-            dst_ref=top_all.at[source],
-            send_sem=down_send.at[step],
-            recv_sem=down_recv.at[source],
-            device_id=(me, source),
-            device_id_type=MESH,
-        ).wait()
-
-    def field_arrived(step):
-        source = other(step)
-        pltpu.make_async_remote_copy(
-            src_ref=field_b.at[source],
-            dst_ref=field_in.at[source],
-            send_sem=field_send.at[step],
-            recv_sem=field_recv.at[source],
-            device_id=(me, source),
-            device_id_type=MESH,
-        ).wait()
-
-    for step in range(1, SHARE):
-        field_arrived(step)
-        down_arrived(step)
-
-    def total(i):
-        value = field_f[col, i]
+        field_copy(step, other(step)).wait()
+
+    for a in range(2):
+        leaf = leaf_f[2 * col + a] + from_top[a]
         for step in range(1, SHARE):
-            value = value + field_in[other(step), i].astype(f32)
-        return value
-
-    pieces = []
-    for q in range(SHARE):
-        tile = top_all[q]
-        pieces += [tile[:, :64], tile[:, 64:]]
-    parent = jnp.concatenate(pieces, axis=0)
-    upper = total(3)
-    down0 = total(4)[:, :64] + wide(nt, parent, tra[0])
-    down1 = upper[:, 64:] + wide(nt, down0, tra[1 + col // 2])
-    down2 = upper[:, :64] + wide(nt, down1, tra[3 + col])
-    down3 = total(2) + wide(nt, down2, tra[pl.ds(7 + 2 * col, 2)].reshape(128, 64))
-    for a in range(2):
-        w = tra[pl.ds(15 + 4 * col + 2 * a, 2)].reshape(128, 64)
-        leaf = total(a) + wide(nt, down3[:, 64 * a : 64 * (a + 1)], w)
+            leaf = leaf + leaf_in[other(step), a].astype(f32)
         b = bas[:, pl.ds(pl.multiple_of(col * 256 + 128 * a, 128), 128)]
         out_ref[:, 128 * a : 128 * (a + 1)] = near_ref[:, 128 * a : 128 * (a + 1)] + nn(
             leaf.astype(bf16), spread(b)
@@ -472,9 +473,13 @@
             pltpu.VMEM((n_leaf, 64, 128), bf16),
             pltpu.VMEM((n_leaf, 64, 128), bf16),
             pltpu.VMEM((64, 128), f32),
+            pltpu.VMEM((7, 256, 128), bf16),
             pltpu.VMEM((8, 128), f32),
-            pltpu.VMEM((n_leaf, 8, 128), f32),
-            pltpu.VMEM((n_leaf, 16, 64), f32),
+            pltpu.VMEM((GROUP, 8, 128), f32),
+            pltpu.VMEM((GROUP, 16, 64), f32),
+            pltpu.VMEM((8, 128), f32),
+            pltpu.VMEM((n_leaf // GROUP, 8, 128), f32),
+            pltpu.VMEM((2 * n_leaf // GROUP, 16, 64), f32),
             pltpu.VMEM((8, 128), f32),
             pltpu.VMEM((SHARE, 8, 128), f32),
             pltpu.VMEM((8, POS), i32),
@@ -484,17 +489,19 @@
             pltpu.VMEM((POS * 64 + 64, 128), f32),
             pltpu.VMEM((POS, 64, 128), bf16),
             pltpu.VMEM((STEPS + 1, 64, 64), f32),
-            pltpu.VMEM((SHARE, PACK, 64, 128), f32),
-            pltpu.VMEM((SHARE, PACK, 64, 128), bf16),
-            pltpu.VMEM((SHARE, PACK, 64, 128), bf16),
+            pltpu.VMEM((B_DEV // 2, 64, 128), f32),
+            pltpu.VMEM((B_DEV // 2, 64, 128), bf16),
+            pltpu.VMEM((SHARE, 2, 64, 128), bf16),
             pltpu.VMEM((64, SHARE * LEAF), f32),
             dma((9,)),
             dma((4,)),
             dma((4,)),
             dma((n_leaf,)),
             dma((n_leaf,)),
-            dma((n_leaf,)),
-            dma((n_leaf,)),
+            dma((GROUP,)),
+            dma((GROUP,)),
+            dma((n_leaf // GROUP,)),
+            dma((n_leaf // GROUP,)),
             dma((SHARE,)),
             dma((SHARE,)),
             dma((SHARE,)),

time: 59.3 us -> 51.5 us (0.87)
  Pallas kernels: 57.7 us -> 49.9 us
    pallas_call x1, Pallas kernels: 57.7 us -> 49.9 us  [body(): pl.pallas_call(functools.partial(kernel, n_leaf), out_shape=jax.ShapeDtyp...]
where the time goes in v2:
time: 51.5 us; the launch traced here: 51.4 us
  Pallas kernels  49.9 us (97%)
  local copies, waits for them, and re-layouts  1.47 us (3%)
    pallas_call x1, Pallas kernels, body(): pl.pallas_call(functools.partial(kernel, n_leaf), out_shape=jax.ShapeDtyp...  49.9 us
    unnamed x1, local copies, waits for them, and re-layouts  1.47 us

profile of v2, /device:TPU:1, one launch (start us, length us, event | category | flops | bytes accessed | tf_op | source)
XLA Modules:
  0.0 51.4 jit_solution(1315173142886711743)
XLA Ops:
  0.0 49.9 %shard_map.100 = f32[64,256]{1,0:T(8,128)} custom-call(bf16[64,1024]{1,0:T(8,128)(2,1)} %bitcast.9, bf16[64,1024]{1,0:T(8,128)(2,1)} %bitcast.10, bf16[64,1024]{1,0:T(8,128)(2,1)} %bitcast.11, bf16[31,64,64]{2,1,0:T(8,128)(2,1)} %tra_h.1, bf16[64,64,256]{2,1,0:T(8,128)(2,1)} %bitcast.7, bf16[62,64,64]{2,1,0:T(8,128)(2,1)} %ttr_h.1, ...), custom_call_target="tpu_custom_call" | custom-call | tf_op jit(solution)/shard_map/pallas_call | solution.py:458
  49.9 1.5 %copy.12 = f32[256,64]{0,1:T(8,128)} copy(f32[256,64]{0,1:T(8,128)} %bitcast.8) | data formatting | bytes 131072

commit v3 on v2

--- a/solution.py
+++ b/solution.py
@@ -62,32 +62,47 @@
     vec_h, emb_h, bas_h, tra_h, cou_h, ttr_h, tco_h, send_boxes, slot_ref, target_ref,
     out_ref,
     vec, emb, bas, tra, cou, ttr, tco,
-    left_box, right_box, outgoing, incoming, root_dup,
+    tiles_out, shares, choice, outgoing, incoming, root_dup, plan_own, plan_in, plan_v, plan_s,
     lifts, top_out, top_in, group_coef, group_out, group_in, upper_coef, top_share, top_all,
     index_v, start_v, index_s, start_s,
     rows_f, blocks, prefix, leaf_f, leaf_b, leaf_in, near_ref,
-    local_sem, halo_send, halo_recv, a2a_send, a2a_recv, top_send, top_recv,
+    local_sem, halo_send, halo_recv, plan_send, plan_recv, ring_send, ring_recv,
+    a2a_send, a2a_recv, top_send, top_recv,
     group_send, group_recv, field_send, field_recv, down_send, down_recv,
 ):
     height = n_leaf.bit_length() - 1
     me = lax.axis_index("leaf")
     col = lax.axis_index("cpl")
 
-    def peer(step):
-        return lax.rem(me + step, n_leaf)
+    group = me // GROUP
+    groups = n_leaf // GROUP
+    inside = lax.rem(me, GROUP)
+    depth_z = GROUP // 2
+    plane = 2 * groups * SHARE
+    z = inside // 2
+    core = lax.rem(inside, 2)
+
+    def leaf_at(x, z_at, c):
+        return x * GROUP + z_at * 2 + c
 
     def other(step):
         return lax.rem(col + step, SHARE)
 
-    barrier = pltpu.get_barrier_semaphore()
-
-    def greet(step, carry):
-        pl.semaphore_signal(barrier, inc=1, device_id=(peer(step), col), device_id_type=MESH)
-        return carry
-
-    lax.fori_loop(1, n_leaf, greet, 0)
-    for step in range(1, SHARE):
-        pl.semaphore_signal(barrier, inc=1, device_id=(me, other(step)), device_id_type=MESH)
+    def mate(step):
+        return lax.rem(inside + step, GROUP)
+
+    def in_plane(r):
+        return (
+            lax.rem(group + r // (2 * SHARE), groups),
+            lax.rem(core + lax.rem(r // SHARE, 2), 2),
+            other(lax.rem(r, SHARE)),
+        )
+
+    def in_column(r):
+        return lax.rem(z + r // SHARE, depth_z), other(lax.rem(r, SHARE))
+
+    next_leaf = lax.rem(me + 1, n_leaf)
+    last_leaf = lax.rem(me + n_leaf - 1, n_leaf)
 
     loads = [
         pltpu.make_async_copy(vec_h, vec.at[:, pl.ds(128, 1024)], local_sem.at[0]),
@@ -98,8 +113,34 @@
         pltpu.make_async_copy(ttr_h, ttr, local_sem.at[5]),
         pltpu.make_async_copy(tco_h, tco, local_sem.at[6]),
     ]
-    for load in loads:
+    for load in loads[:3]:
         load.start()
+
+    barrier = pltpu.get_barrier_semaphore()
+
+    def greet(leaf, cpl):
+        pl.semaphore_signal(barrier, inc=1, device_id=(leaf, cpl), device_id_type=MESH)
+
+    def greet_plane(r, carry):
+        x_at, core_at, cpl_at = in_plane(r)
+        greet(leaf_at(x_at, z, core_at), cpl_at)
+        return carry
+
+    def greet_column(r, carry):
+        z_at, cpl_at = in_column(r)
+        greet(leaf_at(group, z_at, core), cpl_at)
+        return carry
+
+    def greet_mate(step, carry):
+        greet(group * GROUP + mate(step), col)
+        return carry
+
+    lax.fori_loop(1, plane, greet_plane, 0)
+    lax.fori_loop(SHARE, depth_z * SHARE, greet_column, 0)
+    lax.fori_loop(1, GROUP, greet_mate, 0)
+    greet(next_leaf, col)
+    greet(last_leaf, col)
+    greetings = plane - 1 + (depth_z - 1) * SHARE + GROUP - 1 + 2
 
     loads[0].wait()
     loads[1].wait()
@@ -109,17 +150,60 @@
         tiles.append(nt(v, spread(bas[:, 128 * j : 128 * (j + 1)])))
 
     def keep_pair(first, tile):
-        rounded = tile.astype(bf16)
-        turned = pltpu.roll(rounded, 64, 1)
-        left_box[first] = rounded
-        right_box[first] = turned
-        left_box[first + 1] = turned
-        right_box[first + 1] = rounded
-
-    loads[2].wait()
+        tiles_out[(first + 1) // 2] = tile.astype(bf16)
+
     first = B_DEV - 1
     for j, tile in enumerate(tiles):
         keep_pair(first + 2 * j, tile)
+    loads[2].wait()
+    for load in loads[3:]:
+        load.start()
+
+    pl.semaphore_wait(barrier, greetings)
+
+    quarter = pl.multiple_of(col * 16, 16)
+
+    def ring_copy(hop, way, tiles_at, source, src):
+        return pltpu.make_async_remote_copy(
+            src_ref=src,
+            dst_ref=shares.at[source, tiles_at],
+            send_sem=ring_send.at[way, hop],
+            recv_sem=ring_recv.at[source],
+            device_id=(leaf_at(group, lax.rem(z + (1, depth_z - 1)[way], depth_z), core), col),
+            device_id_type=MESH,
+        )
+
+    hops = (depth_z // 2, depth_z // 2 - 1)
+
+    def ring_own(tiles_at):
+        for way in range(2):
+            if hops[way] > 0:
+                ring_copy(
+                    0, way, tiles_at, z, tiles_out.at[tiles_at, pl.ds(quarter, 16)]
+                ).start()
+
+    ring_own(pl.ds(8, 8))
+
+    plan_own[...] = send_boxes[0]
+
+    def plan_copy(r, z_at, cpl_at):
+        z_to, cpl_to = in_column(r)
+        return pltpu.make_async_remote_copy(
+            src_ref=plan_own,
+            dst_ref=plan_in.at[cpl_at, pl.ds(z_at, 1)],
+            send_sem=plan_send.at[r],
+            recv_sem=plan_recv.at[cpl_at * depth_z + z_at],
+            device_id=(leaf_at(group, z_to, core), cpl_to),
+            device_id_type=MESH,
+        )
+
+    def give_plan(r, carry):
+        plan_copy(r, z, col).start()
+        return carry
+
+    lax.fori_loop(1, depth_z * SHARE, give_plan, 0)
+    plan_in[col, pl.ds(z, 1)] = plan_own[...]
+
     while len(tiles) > 1:
         raised = []
         for j in range(len(tiles) // 2):
@@ -134,24 +218,16 @@
             keep_pair(first + 2 * j, tile)
     w = tra[1:3].reshape(128, 64)
     root = wide(nn, tiles[0], jnp.concatenate([w, w], axis=1))
-    left_box[0] = root.astype(bf16)
-    right_box[0] = root.astype(bf16)
-
-    pl.semaphore_wait(barrier, n_leaf - 1 + SHARE - 1)
-
-    group = me // GROUP
-    groups = n_leaf // GROUP
-    inside = lax.rem(me, GROUP)
+    tiles_out[0] = root.astype(bf16)
+    ring_own(pl.ds(0, 8))
+    shares[z] = tiles_out[:, pl.ds(quarter, 16)]
+
     w = tra[0]
     root_dup[...] = wide(nn, root[:, :64], jnp.concatenate([w, w], axis=1))
-    quarter = pl.multiple_of(col * 16, 16)
     half8 = lane_of((8, 128)) < 64
     top_out[...] = jnp.where(
         half8, root_dup[pl.ds(quarter, 8), :], root_dup[pl.ds(pl.multiple_of(quarter + 8, 8), 8), :]
     )
-
-    def mate(step):
-        return lax.rem(inside + step, GROUP)
 
     def top_copy(step, source):
         return pltpu.make_async_remote_copy(
@@ -177,36 +253,10 @@
         top_copy(step, inside).start()
     top_in[inside] = top_out[...]
 
-    half = lane_of((64, 128)) < 64
-
-    def a2a_copy(step):
-        return pltpu.make_async_remote_copy(
-            src_ref=outgoing.at[step],
-            dst_ref=incoming.at[me],
-            send_sem=a2a_send.at[step],
-            recv_sem=a2a_recv.at[me],
-            device_id=(peer(step), col),
-            device_id_type=MESH,
-        )
-
-    def pick(d):
-        return jnp.where(
-            half, left_box[send_boxes[0, 0, 2 * d]], right_box[send_boxes[0, 0, 2 * d + 1]]
-        )
-
-    def give(i, carry):
-        step = lax.rem((i // 2 + 1) * (1 - 2 * lax.rem(i, 2)) + n_leaf, n_leaf)
-        outgoing[step] = pick(peer(step))
-        a2a_copy(step).start()
-        return carry
-
-    lax.fori_loop(0, n_leaf - 1, give, 0)
-    incoming[me] = pick(me)
-
     halos = []
     for k, (src_h, dst) in enumerate(((vec_h, vec), (emb_h, emb))):
         for side, (lanes, to, at) in enumerate(
-            ((pl.ds(896, 128), peer(1), 0), (pl.ds(0, 128), peer(n_leaf - 1), 1152))
+            ((pl.ds(896, 128), next_leaf, 0), (pl.ds(0, 128), last_leaf, 1152))
         ):
             halos.append(
                 pltpu.make_async_remote_copy(
@@ -219,6 +269,67 @@
                 )
             )
             halos[-1].start()
+
+    def plan_wait(r, carry):
+        z_at, cpl_at = in_column(r)
+        plan_copy(r, z_at, cpl_at).wait()
+        return carry
+
+    lax.fori_loop(1, depth_z * SHARE, plan_wait, 0)
+    box = plan_in[...].reshape(SHARE * depth_z, 2 * n_leaf)
+    even_box = box - (box // 2) * 2 == 0
+    even_slot = lax.rem(lane_of(box.shape), 2) == 0
+    plan_v[...] = (box + 1) // 2 + jnp.where(even_box == even_slot, 16, 0)
+    plan_done = pltpu.make_async_copy(plan_v, plan_s, local_sem.at[9])
+    plan_done.start()
+    half = lane_of((16, 128)) < 64
+
+    def take(row, lane):
+        return plan_s[row, lane]
+
+    def give(source):
+        whole = shares[source].reshape(256, 128)
+        choice[0:16] = whole.reshape(16, 16, 128)
+        choice[16:32] = pltpu.roll(whole, 64, 1).reshape(16, 16, 128)
+        place = (group * 2 + core) * depth_z + source
+
+        def pick(leaf_to, cpl_to):
+            row = cpl_to * depth_z + source
+            return jnp.where(
+                half,
+                choice[take(row, 2 * leaf_to)],
+                choice[take(row, 2 * leaf_to + 1)],
+            )
+
+        def send(r, carry):
+            x_to, core_to, cpl_to = in_plane(r)
+            leaf_to = leaf_at(x_to, z, core_to)
+            outgoing[r, source] = pick(leaf_to, cpl_to)
+            pltpu.make_async_remote_copy(
+                src_ref=outgoing.at[r, source],
+                dst_ref=incoming.at[place, pl.ds(quarter, 16)],
+                send_sem=a2a_send.at[r],
+                recv_sem=a2a_recv.at[(group * 2 + core) * SHARE + col],
+                device_id=(leaf_to, cpl_to),
+                device_id_type=MESH,
+            ).start()
+            return carry
+
+        lax.fori_loop(1, plane, send, 0, unroll=4)
+        incoming[place, pl.ds(quarter, 16)] = pick(me, col)
+
+    def ring_step(k):
+        sources = (lax.rem(z + depth_z - k, depth_z), lax.rem(z + k, depth_z))
+        for way in range(2):
+            if k <= hops[way]:
+                everything = pl.ds(0, 16)
+                here = shares.at[sources[way], everything]
+                ring_copy(k - 1, way, everything, sources[way], here).wait()
+                if k < hops[way]:
+                    ring_copy(k, way, everything, sources[way], here).start()
+        for way in range(2):
+            if k <= hops[way]:
+                give(sources[way])
 
     target = target_ref[...]
     slot = slot_ref[...]
@@ -235,7 +346,13 @@
     rank = jnp.sum(member * (earlier + base), axis=0, keepdims=True).astype(i32)
     chosen = rank == row_of((POS, BLK))
     chosen_b = chosen.astype(bf16)
-    pair_row = jnp.broadcast_to((slot // 2).astype(f32), (16, BLK)).astype(bf16)
+    pair_of = slot // 2
+    pair_of = (
+        (pair_of // GROUP) * GROUP
+        + lax.rem(pair_of, 2) * depth_z
+        + lax.rem(pair_of, GROUP) // 2
+    )
+    pair_row = jnp.broadcast_to(pair_of.astype(f32), (16, BLK)).astype(bf16)
     index_v[...] = nt(pair_row, chosen_b)[:8].astype(i32)
     odd = (slot - (slot // 2) * 2).astype(f32)
     odd_col = jnp.sum(jnp.where(chosen, odd, 0.0), axis=1, keepdims=True)
@@ -247,6 +364,9 @@
     ]
     for copy in copies:
         copy.start()
+
+    plan_done.wait()
+    give(z)
 
     def unpack(tile):
         return jnp.concatenate([tile[:, :64], tile[:, 64:]], axis=0)
@@ -272,6 +392,9 @@
         group_copy(step, group).start()
     group_in[group] = group_out[...]
 
+    if hops[0] >= 1:
+        ring_step(1)
+
     loads[4].wait()
 
     def turn(r, carry):
@@ -281,7 +404,10 @@
         rows_f[pl.ds(r + 32, POS, stride=64), :] = d[:, 128:] * used_half
         return carry
 
-    lax.fori_loop(0, 32, turn, 0, unroll=4)
+    lax.fori_loop(0, 16, turn, 0, unroll=4)
+    if hops[0] >= 2:
+        ring_step(2)
+    lax.fori_loop(16, 32, turn, 0, unroll=4)
 
     for step in range(1, groups):
         group_copy(step, lax.rem(group + step, groups)).wait()
@@ -317,11 +443,16 @@
         down_copy(step, col).start()
     top_all[col] = top_share[...]
 
+    if hops[0] >= 3:
+        ring_step(3)
+
     def narrow(j, carry):
         blocks[j] = rows_f[pl.ds(pl.multiple_of(j * 64, 64), 64), :].astype(bf16)
         return carry
 
     lax.fori_loop(0, POS, narrow, 0, unroll=8)
+    if hops[0] >= 4:
+        ring_step(4)
     for copy in copies:
         copy.wait()
 
@@ -367,19 +498,23 @@
         w = tra[pl.ds(15 + 4 * col + 2 * a, 2)].reshape(128, 64)
         from_top.append(wide(nt, parent[:, 64 * a : 64 * (a + 1)], w))
 
-    def arrived(step, carry):
-        source = peer(step)
+    def arrived(r, carry):
+        x_at, core_at, cpl_at = in_plane(r)
+        from_core = x_at * 2 + core_at
         pltpu.make_async_remote_copy(
-            src_ref=outgoing.at[step],
-            dst_ref=incoming.at[source],
-            send_sem=a2a_send.at[step],
-            recv_sem=a2a_recv.at[source],
-            device_id=(source, col),
+            src_ref=outgoing.at[r],
+            dst_ref=incoming.at[
+                pl.ds(pl.multiple_of(from_core * depth_z, depth_z), depth_z),
+                pl.ds(pl.multiple_of(cpl_at * 16, 16), 16),
+            ],
+            send_sem=a2a_send.at[r],
+            recv_sem=a2a_recv.at[from_core * SHARE + cpl_at],
+            device_id=(leaf_at(x_at, z, core_at), cpl_at),
             device_id_type=MESH,
         ).wait()
         return carry
 
-    lax.fori_loop(1, n_leaf, arrived, 0)
+    lax.fori_loop(1, plane, arrived, 0)
 
     prefix[0] = jnp.zeros((64, 64), f32)
 
@@ -451,14 +586,14 @@
 ):
     n_leaf = lax.axis_size("leaf")
     tops = top_transfer.shape[0]
+    plane = 2 * (n_leaf // GROUP) * SHARE
     hbm = pl.BlockSpec(memory_space=pl.ANY)
     vmem = pl.BlockSpec(memory_space=pltpu.VMEM)
-    smem = pl.BlockSpec(memory_space=pltpu.SMEM)
     dma = pltpu.SemaphoreType.DMA
     result = pl.pallas_call(
         functools.partial(kernel, n_leaf),
         out_shape=jax.ShapeDtypeStruct((NRHS, SHARE * LEAF), f32),
-        in_specs=[hbm] * 7 + [smem, vmem, vmem],
+        in_specs=[hbm] * 7 + [vmem] * 3,
         out_specs=vmem,
         scratch_shapes=[
             pltpu.VMEM((64, 1280), bf16),
@@ -468,11 +603,16 @@
             pltpu.VMEM((64, 64, BLK), bf16),
             pltpu.VMEM((tops, 64, 64), bf16),
             pltpu.VMEM((tops, 64, 64), bf16),
-            pltpu.VMEM((BOX, 64, 128), bf16),
-            pltpu.VMEM((BOX, 64, 128), bf16),
-            pltpu.VMEM((n_leaf, 64, 128), bf16),
+            pltpu.VMEM((16, 64, 128), bf16),
+            pltpu.VMEM((GROUP // 2, 16, 16, 128), bf16),
+            pltpu.VMEM((32, 16, 128), bf16),
+            pltpu.VMEM((plane, GROUP // 2, 16, 128), bf16),
             pltpu.VMEM((n_leaf, 64, 128), bf16),
             pltpu.VMEM((64, 128), f32),
+            pltpu.VMEM((1, 2 * n_leaf), i32),
+            pltpu.VMEM((SHARE, GROUP // 2, 2 * n_leaf), i32),
+            pltpu.VMEM((SHARE * GROUP // 2, 2 * n_leaf), i32),
+            pltpu.SMEM((SHARE * GROUP // 2, 2 * n_leaf), i32),
             pltpu.VMEM((7, 256, 128), bf16),
             pltpu.VMEM((8, 128), f32),
             pltpu.VMEM((GROUP, 8, 128), f32),
@@ -493,11 +633,15 @@
             pltpu.VMEM((B_DEV // 2, 64, 128), bf16),
             pltpu.VMEM((SHARE, 2, 64, 128), bf16),
             pltpu.VMEM((64, SHARE * LEAF), f32),
-            dma((9,)),
+            dma((10,)),
             dma((4,)),
             dma((4,)),
-            dma((n_leaf,)),
-            dma((n_leaf,)),
+            dma((SHARE * GROUP // 2,)),
+            dma((SHARE * GROUP // 2,)),
+            dma((2, GROUP // 2)),
+            dma((GROUP // 2,)),
+            dma((plane,)),
+            dma((plane,)),
             dma((GROUP,)),
             dma((GROUP,)),
             dma((n_leaf // GROUP,)),

time: 51.5 us -> 56 us (1.087)
  Pallas kernels: 49.9 us -> 54.3 us
    pallas_call x1, Pallas kernels: 49.9 us -> 54.3 us  [body(): pl.pallas_call(functools.partial(kernel, n_leaf), out_shape=jax.ShapeDtyp...]
where the time goes in v3:
time: 56 us; the launch traced here: 55.8 us
  Pallas kernels  54.3 us (97%)
  local copies, waits for them, and re-layouts  1.47 us (3%)
    pallas_call x1, Pallas kernels, body(): pl.pallas_call(functools.partial(kernel, n_leaf), out_shape=jax.ShapeDtyp...  54.3 us
    unnamed x1, local copies, waits for them, and re-layouts  1.47 us

profile of v3, /device:TPU:1, one launch (start us, length us, event | category | flops | bytes accessed | tf_op | source)
XLA Modules:
  0.0 55.8 jit_solution(1926377222450718803)
XLA Ops:
  0.0 54.3 %shard_map.100 = f32[64,256]{1,0:T(8,128)} custom-call(bf16[64,1024]{1,0:T(8,128)(2,1)} %bitcast.9, bf16[64,1024]{1,0:T(8,128)(2,1)} %bitcast.10, bf16[64,1024]{1,0:T(8,128)(2,1)} %bitcast.11, bf16[31,64,64]{2,1,0:T(8,128)(2,1)} %tra_h.1, bf16[64,64,256]{2,1,0:T(8,128)(2,1)} %bitcast.7, bf16[62,64,64]{2,1,0:T(8,128)(2,1)} %ttr_h.1, ...), custom_call_target="tpu_custom_call" | custom-call | tf_op jit(solution)/shard_map/pallas_call | solution.py:593
  54.4 1.5 %copy.12 = f32[256,64]{0,1:T(8,128)} copy(f32[256,64]{0,1:T(8,128)} %bitcast.8) | data formatting | bytes 131072

commit v4 on v3

--- a/solution.py
+++ b/solution.py
@@ -59,10 +59,10 @@
 
 def kernel(
     n_leaf,
-    vec_h, emb_h, bas_h, tra_h, cou_h, ttr_h, tco_h, send_boxes, slot_ref, target_ref,
+    vec_h, emb_h, bas_h, tra_h, cou_h, ttr_h, tco_h, plan_h, slot_h, target_h,
     out_ref,
     vec, emb, bas, tra, cou, ttr, tco,
-    tiles_out, shares, choice, outgoing, incoming, root_dup, plan_own, plan_in, plan_v, plan_s,
+    tiles_out, shares, choice, outgoing, incoming, root_dup, slot_ref, target_ref, plan_own, plan_in, plan_v, plan_s,
     lifts, top_out, top_in, group_coef, group_out, group_in, upper_coef, top_share, top_all,
     index_v, start_v, index_s, start_s,
     rows_f, blocks, prefix, leaf_f, leaf_b, leaf_in, near_ref,
@@ -113,7 +113,12 @@
         pltpu.make_async_copy(ttr_h, ttr, local_sem.at[5]),
         pltpu.make_async_copy(tco_h, tco, local_sem.at[6]),
     ]
-    for load in loads[:3]:
+    small = [
+        pltpu.make_async_copy(plan_h.at[0], plan_own, local_sem.at[10]),
+        pltpu.make_async_copy(slot_h, slot_ref, local_sem.at[11]),
+        pltpu.make_async_copy(target_h, target_ref, local_sem.at[12]),
+    ]
+    for load in loads[:3] + small:
         load.start()
 
     barrier = pltpu.get_barrier_semaphore()
@@ -135,9 +140,9 @@
         greet(group * GROUP + mate(step), col)
         return carry
 
-    lax.fori_loop(1, plane, greet_plane, 0)
-    lax.fori_loop(SHARE, depth_z * SHARE, greet_column, 0)
-    lax.fori_loop(1, GROUP, greet_mate, 0)
+    lax.fori_loop(1, plane, greet_plane, 0, unroll=True)
+    lax.fori_loop(SHARE, depth_z * SHARE, greet_column, 0, unroll=True)
+    lax.fori_loop(1, GROUP, greet_mate, 0, unroll=True)
     greet(next_leaf, col)
     greet(last_leaf, col)
     greetings = plane - 1 + (depth_z - 1) * SHARE + GROUP - 1 + 2
@@ -158,51 +163,6 @@
     loads[2].wait()
     for load in loads[3:]:
         load.start()
-
-    pl.semaphore_wait(barrier, greetings)
-
-    quarter = pl.multiple_of(col * 16, 16)
-
-    def ring_copy(hop, way, tiles_at, source, src):
-        return pltpu.make_async_remote_copy(
-            src_ref=src,
-            dst_ref=shares.at[source, tiles_at],
-            send_sem=ring_send.at[way, hop],
-            recv_sem=ring_recv.at[source],
-            device_id=(leaf_at(group, lax.rem(z + (1, depth_z - 1)[way], depth_z), core), col),
-            device_id_type=MESH,
-        )
-
-    hops = (depth_z // 2, depth_z // 2 - 1)
-
-    def ring_own(tiles_at):
-        for way in range(2):
-            if hops[way] > 0:
-                ring_copy(
-                    0, way, tiles_at, z, tiles_out.at[tiles_at, pl.ds(quarter, 16)]
-                ).start()
-
-    ring_own(pl.ds(8, 8))
-
-    plan_own[...] = send_boxes[0]
-
-    def plan_copy(r, z_at, cpl_at):
-        z_to, cpl_to = in_column(r)
-        return pltpu.make_async_remote_copy(
-            src_ref=plan_own,
-            dst_ref=plan_in.at[cpl_at, pl.ds(z_at, 1)],
-            send_sem=plan_send.at[r],
-            recv_sem=plan_recv.at[cpl_at * depth_z + z_at],
-            device_id=(leaf_at(group, z_to, core), cpl_to),
-            device_id_type=MESH,
-        )
-
-    def give_plan(r, carry):
-        plan_copy(r, z, col).start()
-        return carry
-
-    lax.fori_loop(1, depth_z * SHARE, give_plan, 0)
-    plan_in[col, pl.ds(z, 1)] = plan_own[...]
 
     while len(tiles) > 1:
         raised = []
@@ -219,8 +179,51 @@
     w = tra[1:3].reshape(128, 64)
     root = wide(nn, tiles[0], jnp.concatenate([w, w], axis=1))
     tiles_out[0] = root.astype(bf16)
-    ring_own(pl.ds(0, 8))
+    pl.semaphore_wait(barrier, greetings)
+
+    quarter = pl.multiple_of(col * 16, 16)
+
+    def ring_copy(hop, way, tiles_at, source, src):
+        return pltpu.make_async_remote_copy(
+            src_ref=src,
+            dst_ref=shares.at[source, tiles_at],
+            send_sem=ring_send.at[way, hop],
+            recv_sem=ring_recv.at[source],
+            device_id=(leaf_at(group, lax.rem(z + (1, depth_z - 1)[way], depth_z), core), col),
+            device_id_type=MESH,
+        )
+
+    hops = (depth_z // 2, depth_z // 2 - 1)
+
+    def ring_own(tiles_at):
+        for way in range(2):
+            if hops[way] > 0:
+                ring_copy(
+                    0, way, tiles_at, z, tiles_out.at[tiles_at, pl.ds(quarter, 16)]
+                ).start()
+
+    ring_own(pl.ds(0, 16))
     shares[z] = tiles_out[:, pl.ds(quarter, 16)]
+
+    small[0].wait()
+
+    def plan_copy(r, z_at, cpl_at):
+        z_to, cpl_to = in_column(r)
+        return pltpu.make_async_remote_copy(
+            src_ref=plan_own,
+            dst_ref=plan_in.at[cpl_at, pl.ds(z_at, 1)],
+            send_sem=plan_send.at[r],
+            recv_sem=plan_recv.at[cpl_at * depth_z + z_at],
+            device_id=(leaf_at(group, z_to, core), cpl_to),
+            device_id_type=MESH,
+        )
+
+    def give_plan(r, carry):
+        plan_copy(r, z, col).start()
+        return carry
+
+    lax.fori_loop(1, depth_z * SHARE, give_plan, 0, unroll=True)
+    plan_in[col, pl.ds(z, 1)] = plan_own[...]
 
     w = tra[0]
     root_dup[...] = wide(nn, root[:, :64], jnp.concatenate([w, w], axis=1))
@@ -275,13 +278,6 @@
         plan_copy(r, z_at, cpl_at).wait()
         return carry
 
-    lax.fori_loop(1, depth_z * SHARE, plan_wait, 0)
-    box = plan_in[...].reshape(SHARE * depth_z, 2 * n_leaf)
-    even_box = box - (box // 2) * 2 == 0
-    even_slot = lax.rem(lane_of(box.shape), 2) == 0
-    plan_v[...] = (box + 1) // 2 + jnp.where(even_box == even_slot, 16, 0)
-    plan_done = pltpu.make_async_copy(plan_v, plan_s, local_sem.at[9])
-    plan_done.start()
     half = lane_of((16, 128)) < 64
 
     def take(row, lane):
@@ -315,7 +311,7 @@
             ).start()
             return carry
 
-        lax.fori_loop(1, plane, send, 0, unroll=4)
+        lax.fori_loop(1, plane, send, 0, unroll=31)
         incoming[place, pl.ds(quarter, 16)] = pick(me, col)
 
     def ring_step(k):
@@ -331,6 +327,15 @@
             if k <= hops[way]:
                 give(sources[way])
 
+    lax.fori_loop(1, depth_z * SHARE, plan_wait, 0)
+    box = plan_in[...].reshape(SHARE * depth_z, 2 * n_leaf)
+    even_box = box - (box // 2) * 2 == 0
+    even_slot = lax.rem(lane_of(box.shape), 2) == 0
+    plan_v[...] = (box + 1) // 2 + jnp.where(even_box == even_slot, 16, 0)
+    plan_done = pltpu.make_async_copy(plan_v, plan_s, local_sem.at[9])
+    plan_done.start()
+    small[1].wait()
+    small[2].wait()
     target = target_ref[...]
     slot = slot_ref[...]
     member = (target == row_of((32, BLK))).astype(f32)
@@ -368,6 +373,9 @@
     plan_done.wait()
     give(z)
 
+    if hops[0] >= 1:
+        ring_step(1)
+
     def unpack(tile):
         return jnp.concatenate([tile[:, :64], tile[:, 64:]], axis=0)
 
@@ -392,22 +400,27 @@
         group_copy(step, group).start()
     group_in[group] = group_out[...]
 
-    if hops[0] >= 1:
-        ring_step(1)
+    if hops[0] >= 2:
+        ring_step(2)
 
     loads[4].wait()
 
     def turn(r, carry):
         x, y = cou[r], cou[r + 32]
         d = nt(chosen_b, jnp.concatenate([x, x, y, y], axis=0))
-        rows_f[pl.ds(r, POS, stride=64), :] = d[:, :128] * used_half
-        rows_f[pl.ds(r + 32, POS, stride=64), :] = d[:, 128:] * used_half
+        rows_f[pl.ds(r, POS, stride=65), :] = d[:, :128] * used_half
+        rows_f[pl.ds(r + 32, POS, stride=65), :] = d[:, 128:] * used_half
         return carry
 
     lax.fori_loop(0, 16, turn, 0, unroll=4)
-    if hops[0] >= 2:
-        ring_step(2)
+
+    if hops[0] >= 3:
+        ring_step(3)
+
     lax.fori_loop(16, 32, turn, 0, unroll=4)
+
+    if hops[0] >= 4:
+        ring_step(4)
 
     for step in range(1, groups):
         group_copy(step, lax.rem(group + step, groups)).wait()
@@ -443,19 +456,11 @@
         down_copy(step, col).start()
     top_all[col] = top_share[...]
 
-    if hops[0] >= 3:
-        ring_step(3)
-
     def narrow(j, carry):
-        blocks[j] = rows_f[pl.ds(pl.multiple_of(j * 64, 64), 64), :].astype(bf16)
+        blocks[j] = rows_f[pl.ds(j * 65, 64), :].astype(bf16)
         return carry
 
     lax.fori_loop(0, POS, narrow, 0, unroll=8)
-    if hops[0] >= 4:
-        ring_step(4)
-    for copy in copies:
-        copy.wait()
-
     loads[3].wait()
     for halo in halos:
         halo.wait()
@@ -498,6 +503,10 @@
         w = tra[pl.ds(15 + 4 * col + 2 * a, 2)].reshape(128, 64)
         from_top.append(wide(nt, parent[:, 64 * a : 64 * (a + 1)], w))
 
+    for copy in copies:
+        copy.wait()
+
+
     def arrived(r, carry):
         x_at, core_at, cpl_at = in_plane(r)
         from_core = x_at * 2 + core_at
@@ -593,7 +602,7 @@
     result = pl.pallas_call(
         functools.partial(kernel, n_leaf),
         out_shape=jax.ShapeDtypeStruct((NRHS, SHARE * LEAF), f32),
-        in_specs=[hbm] * 7 + [vmem] * 3,
+        in_specs=[hbm] * 10,
         out_specs=vmem,
         scratch_shapes=[
             pltpu.VMEM((64, 1280), bf16),
@@ -609,6 +618,8 @@
             pltpu.VMEM((plane, GROUP // 2, 16, 128), bf16),
             pltpu.VMEM((n_leaf, 64, 128), bf16),
             pltpu.VMEM((64, 128), f32),
+            pltpu.VMEM((1, BLK), i32),
+            pltpu.VMEM((1, BLK), i32),
             pltpu.VMEM((1, 2 * n_leaf), i32),
             pltpu.VMEM((SHARE, GROUP // 2, 2 * n_leaf), i32),
             pltpu.VMEM((SHARE * GROUP // 2, 2 * n_leaf), i32),
@@ -626,14 +637,14 @@
             pltpu.VMEM((32, 128), i32),
             pltpu.SMEM((8, POS), i32),
             pltpu.SMEM((32, 128), i32),
-            pltpu.VMEM((POS * 64 + 64, 128), f32),
+            pltpu.VMEM((POS * 65 + 65, 128), f32),
             pltpu.VMEM((POS, 64, 128), bf16),
             pltpu.VMEM((STEPS + 1, 64, 64), f32),
             pltpu.VMEM((B_DEV // 2, 64, 128), f32),
             pltpu.VMEM((B_DEV // 2, 64, 128), bf16),
             pltpu.VMEM((SHARE, 2, 64, 128), bf16),
             pltpu.VMEM((64, SHARE * LEAF), f32),
-            dma((10,)),
+            dma((13,)),
             dma((4,)),
             dma((4,)),
             dma((SHARE * GROUP // 2,)),

time: 56 us -> 46.8 us (0.84)
  Pallas kernels: 54.3 us -> 45.2 us
    pallas_call x1, Pallas kernels: 54.3 us -> 45.2 us  [body(): pl.pallas_call(functools.partial(kernel, n_leaf), out_shape=jax.ShapeDtyp...]
where the time goes in v4:
time: 46.8 us; the launch traced here: 46.7 us
  Pallas kernels  45.2 us (97%)
  local copies, waits for them, and re-layouts  1.47 us (3%)
    pallas_call x1, Pallas kernels, body(): pl.pallas_call(functools.partial(kernel, n_leaf), out_shape=jax.ShapeDtyp...  45.2 us
    unnamed x1, local copies, waits for them, and re-layouts  1.47 us

profile of v4, /device:TPU:1, one launch (start us, length us, event | category | flops | bytes accessed | tf_op | source)
XLA Modules:
  0.0 46.7 jit_solution(18133961486595758860)
XLA Ops:
  0.0 45.2 %shard_map.100 = f32[64,256]{1,0:T(8,128)} custom-call(bf16[64,1024]{1,0:T(8,128)(2,1)} %bitcast.9, bf16[64,1024]{1,0:T(8,128)(2,1)} %bitcast.10, bf16[64,1024]{1,0:T(8,128)(2,1)} %bitcast.11, bf16[31,64,64]{2,1,0:T(8,128)(2,1)} %tra_h.1, bf16[64,64,256]{2,1,0:T(8,128)(2,1)} %bitcast.7, bf16[62,64,64]{2,1,0:T(8,128)(2,1)} %ttr_h.1, ...), custom_call_target="tpu_custom_call" | custom-call | tf_op jit(solution)/shard_map/pallas_call | solution.py:602
  45.2 1.5 %copy.12 = f32[256,64]{0,1:T(8,128)} copy(f32[256,64]{0,1:T(8,128)} %bitcast.8) | data formatting | bytes 131072

commit v5 on v4

--- a/solution.py
+++ b/solution.py
@@ -17,6 +17,8 @@
 POS = 288
 STEPS = POS // 2
 GROUP = 16
+DEPTH = 8
+NEAR_Z = (0, -1, 1, -2, 2, -3, 3)
 
 MESH = pl.DeviceIdType.MESH
 f32, bf16, i32 = jnp.float32, jnp.bfloat16, jnp.int32
@@ -77,7 +79,7 @@
     group = me // GROUP
     groups = n_leaf // GROUP
     inside = lax.rem(me, GROUP)
-    depth_z = GROUP // 2
+    depth_z = DEPTH
     plane = 2 * groups * SHARE
     z = inside // 2
     core = lax.rem(inside, 2)
@@ -98,8 +100,10 @@
             other(lax.rem(r, SHARE)),
         )
 
-    def in_column(r):
-        return lax.rem(z + r // SHARE, depth_z), other(lax.rem(r, SHARE))
+    def z_by(step):
+        return lax.rem(z + step + depth_z, depth_z)
+
+    far = 2 * core - 1
 
     next_leaf = lax.rem(me + 1, n_leaf)
     last_leaf = lax.rem(me + n_leaf - 1, n_leaf)
@@ -121,6 +125,8 @@
     for load in loads[:3] + small:
         load.start()
 
+    plan_in[...] = jnp.zeros_like(plan_in)
+
     barrier = pltpu.get_barrier_semaphore()
 
     def greet(leaf, cpl):
@@ -131,21 +137,21 @@
         greet(leaf_at(x_at, z, core_at), cpl_at)
         return carry
 
-    def greet_column(r, carry):
-        z_at, cpl_at = in_column(r)
-        greet(leaf_at(group, z_at, core), cpl_at)
+    def greet_beside(r, carry):
+        x_at, core_at, cpl_at = in_plane(r)
+        greet(leaf_at(x_at, z_by(1 - 2 * core_at), core_at), cpl_at)
         return carry
 
-    def greet_mate(step, carry):
+    lax.fori_loop(1, plane, greet_plane, 0, unroll=True)
+    lax.fori_loop(0, plane, greet_beside, 0, unroll=True)
+    for step in range(SHARE):
+        for hop in NEAR_Z[1:]:
+            greet(leaf_at(group, z_by(hop), core), other(step))
+    for step in range(1, GROUP):
         greet(group * GROUP + mate(step), col)
-        return carry
-
-    lax.fori_loop(1, plane, greet_plane, 0, unroll=True)
-    lax.fori_loop(SHARE, depth_z * SHARE, greet_column, 0, unroll=True)
-    lax.fori_loop(1, GROUP, greet_mate, 0, unroll=True)
     greet(next_leaf, col)
     greet(last_leaf, col)
-    greetings = plane - 1 + (depth_z - 1) * SHARE + GROUP - 1 + 2
+    greetings = 2 * plane - 1 + (len(NEAR_Z) - 1) * SHARE + GROUP - 1 + 2
 
     loads[0].wait()
     loads[1].wait()
@@ -183,47 +189,38 @@
 
     quarter = pl.multiple_of(col * 16, 16)
 
-    def ring_copy(hop, way, tiles_at, source, src):
+    def ring_copy(place, src):
+        way = lax.rem(place + 1, 2)
         return pltpu.make_async_remote_copy(
             src_ref=src,
-            dst_ref=shares.at[source, tiles_at],
-            send_sem=ring_send.at[way, hop],
-            recv_sem=ring_recv.at[source],
-            device_id=(leaf_at(group, lax.rem(z + (1, depth_z - 1)[way], depth_z), core), col),
+            dst_ref=shares.at[place],
+            send_sem=ring_send.at[place],
+            recv_sem=ring_recv.at[place],
+            device_id=(leaf_at(group, z_by(1 - 2 * way), core), col),
             device_id_type=MESH,
         )
 
-    hops = (depth_z // 2, depth_z // 2 - 1)
-
-    def ring_own(tiles_at):
-        for way in range(2):
-            if hops[way] > 0:
-                ring_copy(
-                    0, way, tiles_at, z, tiles_out.at[tiles_at, pl.ds(quarter, 16)]
-                ).start()
-
-    ring_own(pl.ds(0, 16))
-    shares[z] = tiles_out[:, pl.ds(quarter, 16)]
+    own_share = tiles_out.at[:, pl.ds(quarter, 16)]
+    for place in (1, 2):
+        ring_copy(place, own_share).start()
+    shares[0] = tiles_out[:, pl.ds(quarter, 16)]
 
     small[0].wait()
 
-    def plan_copy(r, z_at, cpl_at):
-        z_to, cpl_to = in_column(r)
+    def plan_copy(place, step, cpl_at):
         return pltpu.make_async_remote_copy(
             src_ref=plan_own,
-            dst_ref=plan_in.at[cpl_at, pl.ds(z_at, 1)],
-            send_sem=plan_send.at[r],
-            recv_sem=plan_recv.at[cpl_at * depth_z + z_at],
-            device_id=(leaf_at(group, z_to, core), cpl_to),
+            dst_ref=plan_in.at[cpl_at, pl.ds(place, 1)],
+            send_sem=plan_send.at[place * SHARE + step],
+            recv_sem=plan_recv.at[cpl_at * DEPTH + place],
+            device_id=(leaf_at(group, z_by(-NEAR_Z[place]), core), other(step)),
             device_id_type=MESH,
         )
 
-    def give_plan(r, carry):
-        plan_copy(r, z, col).start()
-        return carry
-
-    lax.fori_loop(1, depth_z * SHARE, give_plan, 0, unroll=True)
-    plan_in[col, pl.ds(z, 1)] = plan_own[...]
+    plan_pairs = [(p, step) for p in range(len(NEAR_Z)) for step in range(SHARE) if p + step > 0]
+    for place, step in plan_pairs:
+        plan_copy(place, step, col).start()
+    plan_in[col, 0:1] = plan_own[...]
 
     w = tra[0]
     root_dup[...] = wide(nn, root[:, :64], jnp.concatenate([w, w], axis=1))
@@ -273,67 +270,45 @@
             )
             halos[-1].start()
 
-    def plan_wait(r, carry):
-        z_at, cpl_at = in_column(r)
-        plan_copy(r, z_at, cpl_at).wait()
-        return carry
-
     half = lane_of((16, 128)) < 64
 
     def take(row, lane):
         return plan_s[row, lane]
 
-    def give(source):
-        whole = shares[source].reshape(256, 128)
+    def ready(place):
+        whole = shares[place].reshape(256, 128)
         choice[0:16] = whole.reshape(16, 16, 128)
         choice[16:32] = pltpu.roll(whole, 64, 1).reshape(16, 16, 128)
-        place = (group * 2 + core) * depth_z + source
+
+    def give(place, kind):
+        slot_at = place if kind == 0 else DEPTH - 1
+        to_z = z_by(far * kind)
+        from_core = group * 2 + core
 
         def pick(leaf_to, cpl_to):
-            row = cpl_to * depth_z + source
+            row = cpl_to * DEPTH + place
             return jnp.where(
-                half,
-                choice[take(row, 2 * leaf_to)],
-                choice[take(row, 2 * leaf_to + 1)],
+                half, choice[take(row, 2 * leaf_to)], choice[take(row, 2 * leaf_to + 1)]
             )
 
         def send(r, carry):
             x_to, core_to, cpl_to = in_plane(r)
-            leaf_to = leaf_at(x_to, z, core_to)
-            outgoing[r, source] = pick(leaf_to, cpl_to)
+            leaf_to = leaf_at(x_to, to_z, core_to)
+            outgoing[r, slot_at] = pick(leaf_to, cpl_to)
             pltpu.make_async_remote_copy(
-                src_ref=outgoing.at[r, source],
-                dst_ref=incoming.at[place, pl.ds(quarter, 16)],
-                send_sem=a2a_send.at[r],
-                recv_sem=a2a_recv.at[(group * 2 + core) * SHARE + col],
+                src_ref=outgoing.at[r, slot_at],
+                dst_ref=incoming.at[from_core * DEPTH + slot_at, pl.ds(quarter, 16)],
+                send_sem=a2a_send.at[kind, r],
+                recv_sem=a2a_recv.at[kind, from_core * SHARE + col],
                 device_id=(leaf_to, cpl_to),
                 device_id_type=MESH,
             ).start()
             return carry
 
-        lax.fori_loop(1, plane, send, 0, unroll=31)
-        incoming[place, pl.ds(quarter, 16)] = pick(me, col)
-
-    def ring_step(k):
-        sources = (lax.rem(z + depth_z - k, depth_z), lax.rem(z + k, depth_z))
-        for way in range(2):
-            if k <= hops[way]:
-                everything = pl.ds(0, 16)
-                here = shares.at[sources[way], everything]
-                ring_copy(k - 1, way, everything, sources[way], here).wait()
-                if k < hops[way]:
-                    ring_copy(k, way, everything, sources[way], here).start()
-        for way in range(2):
-            if k <= hops[way]:
-                give(sources[way])
-
-    lax.fori_loop(1, depth_z * SHARE, plan_wait, 0)
-    box = plan_in[...].reshape(SHARE * depth_z, 2 * n_leaf)
-    even_box = box - (box // 2) * 2 == 0
-    even_slot = lax.rem(lane_of(box.shape), 2) == 0
-    plan_v[...] = (box + 1) // 2 + jnp.where(even_box == even_slot, 16, 0)
-    plan_done = pltpu.make_async_copy(plan_v, plan_s, local_sem.at[9])
-    plan_done.start()
+        lax.fori_loop(1 if kind == 0 else 0, plane, send, 0, unroll=True)
+        if kind == 0:
+            incoming[from_core * DEPTH + slot_at, pl.ds(quarter, 16)] = pick(me, col)
+
     small[1].wait()
     small[2].wait()
     target = target_ref[...]
@@ -352,10 +327,12 @@
     chosen = rank == row_of((POS, BLK))
     chosen_b = chosen.astype(bf16)
     pair_of = slot // 2
+    apart = lax.rem(lax.rem(pair_of, GROUP) // 2 - z + depth_z, depth_z)
+    place_of = jnp.where(apart < depth_z // 2, 2 * apart, 2 * (depth_z - apart) - 1)
     pair_of = (
         (pair_of // GROUP) * GROUP
         + lax.rem(pair_of, 2) * depth_z
-        + lax.rem(pair_of, GROUP) // 2
+        + place_of
     )
     pair_row = jnp.broadcast_to(pair_of.astype(f32), (16, BLK)).astype(bf16)
     index_v[...] = nt(pair_row, chosen_b)[:8].astype(i32)
@@ -370,11 +347,24 @@
     for copy in copies:
         copy.start()
 
+    for place, step in plan_pairs:
+        plan_copy(place, step, other(step)).wait()
+    box = plan_in[...].reshape(SHARE * depth_z, 2 * n_leaf)
+    even_box = box - (box // 2) * 2 == 0
+    even_slot = lax.rem(lane_of(box.shape), 2) == 0
+    plan_v[...] = (box + 1) // 2 + jnp.where(even_box == even_slot, 16, 0)
+    plan_done = pltpu.make_async_copy(plan_v, plan_s, local_sem.at[9])
+    plan_done.start()
+    for place in (1, 2):
+        ring_copy(place, own_share).wait()
+        ring_copy(place + 2, shares.at[place]).start()
     plan_done.wait()
-    give(z)
-
-    if hops[0] >= 1:
-        ring_step(1)
+    ready(0)
+    give(0, 0)
+
+    for place in (1, 2):
+        ready(place)
+        give(place, 0)
 
     def unpack(tile):
         return jnp.concatenate([tile[:, :64], tile[:, 64:]], axis=0)
@@ -400,8 +390,12 @@
         group_copy(step, group).start()
     group_in[group] = group_out[...]
 
-    if hops[0] >= 2:
-        ring_step(2)
+    for place in (3, 4):
+        ring_copy(place, shares.at[place - 2]).wait()
+        ring_copy(place + 2, shares.at[place]).start()
+    for place in (3, 4):
+        ready(place)
+        give(place, 0)
 
     loads[4].wait()
 
@@ -412,15 +406,17 @@
         rows_f[pl.ds(r + 32, POS, stride=65), :] = d[:, 128:] * used_half
         return carry
 
-    lax.fori_loop(0, 16, turn, 0, unroll=4)
-
-    if hops[0] >= 3:
-        ring_step(3)
-
-    lax.fori_loop(16, 32, turn, 0, unroll=4)
-
-    if hops[0] >= 4:
-        ring_step(4)
+    lax.fori_loop(0, 16, turn, 0, unroll=8)
+
+    for place in (5, 6):
+        ring_copy(place, shares.at[place - 2]).wait()
+    ready(6 - core)
+    give(6 - core, 1)
+    for place in (5, 6):
+        ready(place)
+        give(place, 0)
+
+    lax.fori_loop(16, 32, turn, 0, unroll=8)
 
     for step in range(1, groups):
         group_copy(step, lax.rem(group + step, groups)).wait()
@@ -507,23 +503,30 @@
         copy.wait()
 
 
-    def arrived(r, carry):
-        x_at, core_at, cpl_at = in_plane(r)
-        from_core = x_at * 2 + core_at
-        pltpu.make_async_remote_copy(
-            src_ref=outgoing.at[r],
-            dst_ref=incoming.at[
-                pl.ds(pl.multiple_of(from_core * depth_z, depth_z), depth_z),
-                pl.ds(pl.multiple_of(cpl_at * 16, 16), 16),
-            ],
-            send_sem=a2a_send.at[r],
-            recv_sem=a2a_recv.at[from_core * SHARE + cpl_at],
-            device_id=(leaf_at(x_at, z, core_at), cpl_at),
-            device_id_type=MESH,
-        ).wait()
-        return carry
-
-    lax.fori_loop(1, plane, arrived, 0)
+    def arrived(kind):
+        def wait(r, carry):
+            x_at, core_at, cpl_at = in_plane(r)
+            from_core = x_at * 2 + core_at
+            many = DEPTH - 1 if kind == 0 else 1
+            slots = pl.ds(kind * (DEPTH - 1), many)
+            first = from_core * DEPTH + kind * (DEPTH - 1)
+            pltpu.make_async_remote_copy(
+                src_ref=outgoing.at[r, slots],
+                dst_ref=incoming.at[
+                    pl.ds(first, many),
+                    pl.ds(pl.multiple_of(cpl_at * 16, 16), 16),
+                ],
+                send_sem=a2a_send.at[kind, r],
+                recv_sem=a2a_recv.at[kind, from_core * SHARE + cpl_at],
+                device_id=(leaf_at(x_at, z_by(far * kind), core_at), cpl_at),
+                device_id_type=MESH,
+            ).wait()
+            return carry
+
+        lax.fori_loop(1 if kind == 0 else 0, plane, wait, 0)
+
+    for kind in range(2):
+        arrived(kind)
 
     prefix[0] = jnp.zeros((64, 64), f32)
 
@@ -539,7 +542,7 @@
         prefix[u + 1] = acc
         return acc
 
-    lax.fori_loop(0, STEPS, couple, jnp.zeros((64, 64), f32), unroll=48)
+    lax.fori_loop(0, STEPS, couple, jnp.zeros((64, 64), f32), unroll=True)
 
     def run(m):
         return jnp.clip(start_s[m, 0], 0, STEPS)
@@ -613,7 +616,7 @@
             pltpu.VMEM((tops, 64, 64), bf16),
             pltpu.VMEM((tops, 64, 64), bf16),
             pltpu.VMEM((16, 64, 128), bf16),
-            pltpu.VMEM((GROUP // 2, 16, 16, 128), bf16),
+            pltpu.VMEM((7, 16, 16, 128), bf16),
             pltpu.VMEM((32, 16, 128), bf16),
             pltpu.VMEM((plane, GROUP // 2, 16, 128), bf16),
             pltpu.VMEM((n_leaf, 64, 128), bf16),
@@ -647,12 +650,12 @@
             dma((13,)),
             dma((4,)),
             dma((4,)),
-            dma((SHARE * GROUP // 2,)),
-            dma((SHARE * GROUP // 2,)),
-            dma((2, GROUP // 2)),
-            dma((GROUP // 2,)),
-            dma((plane,)),
-            dma((plane,)),
+            dma((7 * SHARE,)),
+            dma((SHARE * DEPTH,)),
+            dma((7,)),
+            dma((7,)),
+            dma((2, plane)),
+            dma((2, plane)),
             dma((GROUP,)),
             dma((GROUP,)),
             dma((n_leaf // GROUP,)),

time: 46.8 us -> 45.3 us (0.968)
  Pallas kernels: 45.2 us -> 43.7 us
    pallas_call x1, Pallas kernels: 45.2 us -> 43.7 us  [body(): pl.pallas_call(functools.partial(kernel, n_leaf), out_shape=jax.ShapeDtyp...]
where the time goes in v5:
time: 45.3 us; the launch traced here: 45.2 us
  Pallas kernels  43.7 us (96%)
  local copies, waits for them, and re-layouts  1.47 us (3%)
    pallas_call x1, Pallas kernels, body(): pl.pallas_call(functools.partial(kernel, n_leaf), out_shape=jax.ShapeDtyp...  43.7 us
    unnamed x1, local copies, waits for them, and re-layouts  1.47 us

profile of v5, /device:TPU:1, one launch (start us, length us, event | category | flops | bytes accessed | tf_op | source)
XLA Modules:
  0.0 45.2 jit_solution(3439809317392858667)
XLA Ops:
  0.0 43.7 %shard_map.100 = f32[64,256]{1,0:T(8,128)} custom-call(bf16[64,1024]{1,0:T(8,128)(2,1)} %bitcast.9, bf16[64,1024]{1,0:T(8,128)(2,1)} %bitcast.10, bf16[64,1024]{1,0:T(8,128)(2,1)} %bitcast.11, bf16[31,64,64]{2,1,0:T(8,128)(2,1)} %tra_h.1, bf16[64,64,256]{2,1,0:T(8,128)(2,1)} %bitcast.7, bf16[62,64,64]{2,1,0:T(8,128)(2,1)} %ttr_h.1, ...), custom_call_target="tpu_custom_call" | custom-call | tf_op jit(solution)/shard_map/pallas_call | solution.py:605
  43.7 1.5 %copy.12 = f32[256,64]{0,1:T(8,128)} copy(f32[256,64]{0,1:T(8,128)} %bitcast.8) | data formatting | bytes 131072

commit v6 on v5

--- a/solution.py
+++ b/solution.py
@@ -201,10 +201,6 @@
         )
 
     own_share = tiles_out.at[:, pl.ds(quarter, 16)]
-    for place in (1, 2):
-        ring_copy(place, own_share).start()
-    shares[0] = tiles_out[:, pl.ds(quarter, 16)]
-
     small[0].wait()
 
     def plan_copy(place, step, cpl_at):
@@ -221,6 +217,10 @@
     for place, step in plan_pairs:
         plan_copy(place, step, col).start()
     plan_in[col, 0:1] = plan_own[...]
+
+    for place in (1, 2):
+        ring_copy(place, own_share).start()
+    shares[0] = tiles_out[:, pl.ds(quarter, 16)]
 
     w = tra[0]
     root_dup[...] = wide(nn, root[:, :64], jnp.concatenate([w, w], axis=1))

time: 45.3 us -> 42.9 us (0.947)
  Pallas kernels: 43.7 us -> 41.3 us
    pallas_call x1, Pallas kernels: 43.7 us -> 41.3 us  [body(): pl.pallas_call(functools.partial(kernel, n_leaf), out_shape=jax.ShapeDtyp...]
where the time goes in v6:
time: 42.9 us; the launch traced here: 42.8 us
  Pallas kernels  41.3 us (96%)
  local copies, waits for them, and re-layouts  1.47 us (3%)
    pallas_call x1, Pallas kernels, body(): pl.pallas_call(functools.partial(kernel, n_leaf), out_shape=jax.ShapeDtyp...  41.3 us
    unnamed x1, local copies, waits for them, and re-layouts  1.47 us

profile of v6, /device:TPU:1, one launch (start us, length us, event | category | flops | bytes accessed | tf_op | source)
XLA Modules:
  0.0 42.8 jit_solution(3830513602172990296)
XLA Ops:
  0.0 41.3 %shard_map.100 = f32[64,256]{1,0:T(8,128)} custom-call(bf16[64,1024]{1,0:T(8,128)(2,1)} %bitcast.9, bf16[64,1024]{1,0:T(8,128)(2,1)} %bitcast.10, bf16[64,1024]{1,0:T(8,128)(2,1)} %bitcast.11, bf16[31,64,64]{2,1,0:T(8,128)(2,1)} %tra_h.1, bf16[64,64,256]{2,1,0:T(8,128)(2,1)} %bitcast.7, bf16[62,64,64]{2,1,0:T(8,128)(2,1)} %ttr_h.1, ...), custom_call_target="tpu_custom_call" | custom-call | tf_op jit(solution)/shard_map/pallas_call | solution.py:605
  41.3 1.5 %copy.12 = f32[256,64]{0,1:T(8,128)} copy(f32[256,64]{0,1:T(8,128)} %bitcast.8) | data formatting | bytes 131072
